TPU v7x, 128 devices: a whole 4x4x4 slice. The times are simulated.
128 devices in a mesh: space: 32 (over y, x, core), tm: 4 (over z).
Axes of the slice: x: 4, y: 4, z: 4, core: 2. Of those that a mesh axis runs over, the one named last changes fastest.
Arguments:
- sources: float32 [2, 2, 4, 3, 32, 4, 1024], P(None, None, None, None, 'space', 'tm'), may hold values from -6 to 6
- links: float32 [4, 2, 3, 3, 32, 4, 1024], P(None, None, None, None, 'space', 'tm'), may hold values from -6 to 6
- clover: float32 [2, 2, 6, 6, 32, 4, 1024], P(None, None, None, None, 'space', 'tm'), may hold values from -0.6 to 3.6
- momenta: int32 [33, 3], replicated, may hold values from -3 to 3, as said below
Outputs:
- loops: float32 [2, 32, 33, 4], P(None, 'space', None, 'tm')
Inputs may be any that keep to these rules, and one draw needn't show every extreme that they name: `momenta`: no row is the zero vector.
All inputs are finite; a program needn't handle non-finite values.
Results may differ from a plain program's by a relative error of at most 0.0003.
Values sent between devices are 32-bit elements; how exact they have to be, the bound alone decides.
A program may use at most 192 MiB of HBM per device.

v0:
```python
import math

import jax
import jax.numpy as jnp
import numpy as np
from jax import lax
from jax.experimental import pallas as pl
from jax.experimental.pallas import tpu as pltpu
from jax.sharding import PartitionSpec as P

MESH = pl.DeviceIdType.MESH
NZ = 32
NY = 32
KAPPA = 0.1
MOM = 48


UPPER = (((1, 1), (0, 1)), ((1, 0), (0, 2)), ((0, 1), (1, 3)), ((0, 0), (1, 0)))
LOWER = (((1, 3), (0, 3)), ((1, 2), (0, 0)), ((0, 3), (1, 1)), ((0, 0), (1, 0)))


def gamma_products():
    sigma = [
        np.array([[0, 1], [1, 0]]) + 0j,
        np.array([[0, -1j], [1j, 0]]),
        np.array([[1, 0], [0, -1]]) + 0j,
    ]
    zero = np.zeros((2, 2)) + 0j
    singles = [np.block([[zero, 1j * s], [-1j * s, zero]]) for s in sigma]
    singles.append(np.block([[zero, np.eye(2)], [np.eye(2), zero]]) + 0j)
    products = []
    for bits in range(16):
        product = np.eye(4) + 0j
        for direction in range(4):
            if bits >> direction & 1:
                product = product @ singles[direction]
        products.append(product)
    return products


def times_i(power, re, im):
    power %= 4
    if power == 0:
        return re, im
    if power == 1:
        return -im, re
    if power == 2:
        return -re, -im
    return im, -re


def add_times_i(power, acc, term):
    (ar, ai), (re, im) = acc, term
    power %= 4
    if power == 0:
        return ar + re, ai + im
    if power == 1:
        return ar - im, ai + re
    if power == 2:
        return ar - re, ai - im
    return ar + im, ai - re


def color_apply(link, half, adjoint):
    hr, hi = half
    outr = outi = None
    for b in range(3):
        if adjoint:
            ur, ui = link[0, b], link[1, b]
        else:
            ur, ui = link[0, :, b], link[1, :, b]
        ur, ui = ur[None], ui[None]
        xr, xi = hr[:, b][:, None], hi[:, b][:, None]
        if adjoint:
            tr, ti = ur * xr + ui * xi, ur * xi - ui * xr
        else:
            tr, ti = ur * xr - ui * xi, ur * xi + ui * xr
        outr, outi = (tr, ti) if outr is None else (outr + tr, outi + ti)
    return outr, outi


def clover_apply(mat, fr, fi):
    xr, xi = fr.reshape(2, 6, 8, 128), fi.reshape(2, 6, 8, 128)
    outr = outi = None
    for i in range(6):
        cr, ci = mat[0, :, :, i], mat[1, :, :, i]
        vr, vi = xr[:, i][:, None], xi[:, i][:, None]
        tr, ti = cr * vr - ci * vi, cr * vi + ci * vr
        outr, outi = (tr, ti) if outr is None else (outr + tr, outi + ti)
    return outr.reshape(4, 3, 8, 128), outi.reshape(4, 3, 8, 128)


def kernel(
    n_space, n_tm,
    src_hbm, link_hbm, clov_hbm, mom_ref, out_ref,
    src, link, clov, wlink, wclov, sfield, field, inner, bil, cur, phase_hi, phase_lo, momrow,
    send, recv, norm_a, norm_ar, norm_b, norm_br, norm_t, loop_s, loop_r,
    in_sem, send_sem, recv_sem, norm_ssem, norm_rsem, loop_ssem, loop_rsem,
):
    x = lax.axis_index("space")
    t = lax.axis_index("tm")
    x_up, x_dn = lax.rem(x + 1, n_space), lax.rem(x + n_space - 1, n_space)
    t_up, t_dn = lax.rem(t + 1, n_tm), lax.rem(t + n_tm - 1, n_tm)

    loads = [
        pltpu.make_async_copy(a, b, in_sem.at[k])
        for k, (a, b) in enumerate(((src_hbm, src), (clov_hbm, clov), (link_hbm, link)))
    ]
    for load in loads:
        load.start()

    barrier = pltpu.get_barrier_semaphore()

    def greet_space(d, carry):
        pl.semaphore_signal(barrier, inc=1, device_id=(lax.rem(x + d, n_space), t), device_id_type=MESH)
        return carry

    lax.fori_loop(1, n_space, greet_space, 0)
    for d in range(1, n_tm):
        pl.semaphore_signal(barrier, inc=1, device_id=(x, lax.rem(t + d, n_tm)), device_id_type=MESH)

    lane = lax.broadcasted_iota(jnp.int32, (8, 128), 1)
    row = lax.broadcasted_iota(jnp.int32, (8, 128), 0)
    zc = lane & 31
    yc = row * 4 + (lane >> 5)
    ev = ((yc + zc + x + t) & 1) == 0
    low_rows = row < 4

    def move(v, axis, by):
        if axis == 2:
            last = v.ndim - 1
            if by == 1:
                return jnp.where(zc == 31, pltpu.roll(v, 31, last), pltpu.roll(v, 127, last))
            return jnp.where(zc == 0, pltpu.roll(v, 97, last), pltpu.roll(v, 1, last))
        if by == 1:
            a = pltpu.roll(v, 96, v.ndim - 1)
            return jnp.where(lane >= 96, pltpu.roll(a, 7, v.ndim - 2), a)
        a = pltpu.roll(v, 32, v.ndim - 1)
        return jnp.where(lane < 32, pltpu.roll(a, 1, v.ndim - 2), a)

    mom = mom_ref[...].astype(jnp.float32)
    n_mom = mom.shape[1]
    eye = lax.broadcasted_iota(jnp.int32, (MOM, n_mom), 0) == lax.broadcasted_iota(jnp.int32, (MOM, n_mom), 1)
    columns = [
        jnp.sum(jnp.where(eye, jnp.broadcast_to(mom[k : k + 1], (MOM, n_mom)), 0.0), axis=1, keepdims=True).astype(jnp.int32)
        for k in range(3)
    ]

    def cos_sin(k):
        a = (k - 16).astype(jnp.float32) * (math.pi / 32)
        q = a * a
        s = 1.0 / math.factorial(11)
        for m in (9, 7, 5, 3, 1):
            s = 1.0 / math.factorial(m) - q * s
        s = s * a
        c = 1.0 / math.factorial(12)
        for m in (10, 8, 6, 4, 2, 0):
            c = 1.0 / math.factorial(m) - q * c
        return 2.0 * s * s - 1.0, -2.0 * s * c

    zero_rows = jnp.zeros((64 - MOM, 2048), jnp.bfloat16)
    for ref in (phase_hi, phase_lo):
        ref[MOM:64, :] = zero_rows
        ref[64 + MOM : 128, :] = zero_rows

    lane1 = lax.broadcasted_iota(jnp.int32, (1, 128), 1)

    def phases(s, carry):
        yrow = s * 4 + (lane1 >> 5)
        zrow = lane1 & 31
        k = (columns[0] * x + columns[1] * yrow + columns[2] * zrow) & 31
        c, sn = cos_sin(k)
        for value, places in ((c, ((0, 0, 1), (64, 128, 1))), (sn, ((0, 128, 1), (64, 0, -1)))):
            for r0, c0, sign in places:
                v = value if sign == 1 else -value
                hi = v.astype(jnp.bfloat16)
                at = pl.ds(pl.multiple_of(s * 256 + c0, 128), 128)
                phase_hi[r0 : r0 + MOM, at] = hi
                phase_lo[r0 : r0 + MOM, at] = (v - hi.astype(jnp.float32)).astype(jnp.bfloat16)
        return carry

    lax.fori_loop(0, 8, phases, 0)

    momrow[...] = jnp.zeros_like(momrow)
    momrow[0:1, 0:n_mom] = mom[2:3]
    momrow[0:1, 64 : 64 + n_mom] = mom[2:3]
    loop_s[...] = jnp.zeros_like(loop_s)

    loads[0].wait()
    for re_im in range(2):
        a = src[0, re_im]
        b = move(src[1, re_im], 2, -1)
        sfield[0, re_im] = jnp.where(ev, a, b)
        sfield[1, re_im] = jnp.where(ev, b, a)

    loads[1].wait()

    def pack_clover(k, carry):
        re_im, chi, r = k // 12, (k // 6) % 2, k % 6
        sign = (1 - 2 * re_im).astype(jnp.float32)
        a = clov[re_im, chi, r]
        b = move(a, 2, -1)
        for par, v in ((0, jnp.where(ev, a, b)), (1, jnp.where(ev, b, a))):
            wclov[1, par, re_im, chi, r] = v
            wclov[0, par, re_im, chi, :, r] = v * sign
        return carry

    lax.fori_loop(0, 24, pack_clover, 0)

    loads[2].wait()
    t_sign = jnp.where(t == n_tm - 1, -1.0, 1.0).astype(jnp.float32)

    def pack_links(k, carry):
        mu, re_im = k // 2, k % 2
        a = link[mu, re_im] * jnp.where(mu == 3, t_sign, 1.0)
        b = move(a, 2, -1)
        wlink[0, mu, re_im] = jnp.where(ev, a, b)
        wlink[1, mu, re_im] = jnp.where(ev, b, a)
        return carry

    lax.fori_loop(0, 8, pack_links, 0)

    pl.semaphore_wait(barrier, n_space - 1 + n_tm - 1)

    ROUTES = ((3, -1, (x, t_dn)), (0, -1, (x_dn, t)), (3, 1, (x, t_up)), (0, 1, (x_up, t)))

    def halo(j, k):
        return pltpu.make_async_remote_copy(
            src_ref=send.at[j, k], dst_ref=recv.at[j, k], send_sem=send_sem, recv_sem=recv_sem.at[j, k],
            device_id=ROUTES[k][2], device_id_type=MESH,
        )

    def project(fr, fi, mu, sign):
        rows_r, rows_i = [], []
        for spin in range(2):
            col, power = UPPER[mu][spin]
            if sign < 0:
                power += 2
            r, i = add_times_i(power, (fr[spin], fi[spin]), (fr[2 + col], fi[2 + col]))
            rows_r.append(r)
            rows_i.append(i)
        return jnp.stack(rows_r), jnp.stack(rows_i)

    def add_up(acc, half, mu, sign):
        hr, hi = half
        for spin in range(2):
            acc[spin] = (hr[spin], hi[spin]) if acc[spin] is None else (acc[spin][0] + hr[spin], acc[spin][1] + hi[spin])
            col, power = LOWER[mu][spin]
            if sign < 0:
                power += 2
            term = (hr[col], hi[col])
            acc[2 + spin] = times_i(power, *term) if acc[2 + spin] is None else add_times_i(power, acc[2 + spin], term)

    def hop(j, par, fr, fi, early, late):
        to = 1 - par
        for k, (mu, sign, _) in enumerate(ROUTES):
            half = project(fr, fi, mu, sign)
            if sign > 0:
                half = color_apply(wlink.at[par, mu], half, True)
            send[j, k, 0] = half[0]
            send[j, k, 1] = half[1]
            halo(j, k).start()
        early()
        acc = [None] * 4
        for mu in (1, 2):
            hr, hi = project(fr, fi, mu, -1)
            ahead = (move(hr, mu, 1), move(hi, mu, 1))
            add_up(acc, color_apply(wlink.at[to, mu], ahead, False), mu, -1)
            hr, hi = color_apply(wlink.at[par, mu], project(fr, fi, mu, 1), True)
            add_up(acc, (move(hr, mu, -1), move(hi, mu, -1)), mu, 1)
        late()
        for k, (mu, sign, _) in enumerate(ROUTES):
            halo(j, k).wait_recv()
            half = (recv[j, k, 0], recv[j, k, 1])
            if sign < 0:
                half = color_apply(wlink.at[to, mu], half, False)
            add_up(acc, half, mu, sign)
        return jnp.stack([a[0] for a in acc]), jnp.stack([a[1] for a in acc])

    def norm_local(p, fr, fi):
        sq = jnp.sum(fr * fr + fi * fi, axis=(0, 1))
        e, o = jnp.where(ev, sq, 0.0), jnp.where(ev, 0.0, sq)
        norm_a[p] = jnp.where(low_rows, e + pltpu.roll(e, 4, 0), o + pltpu.roll(o, 4, 0))

    def norm_send_a(p):
        for d in range(1, n_tm):
            pltpu.make_async_remote_copy(
                src_ref=norm_a.at[p], dst_ref=norm_ar.at[p, n_tm - 1 - d], send_sem=norm_ssem.at[p, 0],
                recv_sem=norm_rsem.at[p, 0], device_id=(x, lax.rem(t + d, n_tm)), device_id_type=MESH,
            ).start()

    def norm_recv_a(p):
        whole = norm_ar.at[p]
        pltpu.make_async_copy(whole, whole, norm_rsem.at[p, 0]).wait()
        norm_b[p] = norm_a[p] + jnp.sum(norm_ar[p], axis=0)

    def norm_send_b(p):
        def step(d, carry):
            pltpu.make_async_remote_copy(
                src_ref=norm_b.at[p], dst_ref=norm_br.at[p, n_space - 1 - d], send_sem=norm_ssem.at[p, 1],
                recv_sem=norm_rsem.at[p, 1], device_id=(lax.rem(x + d, n_space), t), device_id_type=MESH,
            ).start()
            return carry

        lax.fori_loop(1, n_space, step, 0)

    def norm_recv_b(p):
        whole = norm_br.at[p]
        pltpu.make_async_copy(whole, whole, norm_rsem.at[p, 1]).wait()
        norm_t[p] = norm_b[p] + jnp.sum(norm_br[p], axis=0)

    def total(p):
        v = norm_t[p]
        both = []
        for part in (jnp.where(low_rows, v, 0.0), jnp.where(low_rows, 0.0, v)):
            both.append(jnp.sum(jnp.sum(part, axis=0, keepdims=True), axis=1, keepdims=True))
        return both

    def spread(pair):
        return jnp.where(ev, jnp.broadcast_to(pair[0], (8, 128)), jnp.broadcast_to(pair[1], (8, 128)))

    products = gamma_products()

    def project_loops(q, at_field, at_inner):
        for a in range(4):
            par_r, par_i = [], []
            for par, ref, at in ((0, field, at_field), (1, inner, at_inner)):
                br = bi = None
                for c in range(3):
                    sr, si = sfield[par, 0, a, c], sfield[par, 1, a, c]
                    pr, pi = ref[at, 0, :, c], ref[at, 1, :, c]
                    tr, ti = sr * pr + si * pi, sr * pi - si * pr
                    br, bi = (tr, ti) if br is None else (br + tr, bi + ti)
                par_r.append(br)
                par_i.append(bi)
            for re_im, (e, o) in enumerate((par_r, par_i)):
                bil[0, re_im, a] = jnp.where(ev, e, o)
                bil[1, re_im, a] = jnp.where(ev, o, e)

        def gammas(n, carry):
            for first in range(4):
                group = [g for g in range(16) if abs(products[g][0, first]) > 0.5]
                perm = [int(np.argmax(np.abs(products[group[0]][a]))) for a in range(4)]
                terms = [(bil[n, 0, a, perm[a]], bil[n, 1, a, perm[a]]) for a in range(4)]
                for g in group:
                    acc = None
                    for a in range(4):
                        power = int(round(np.angle(products[g][a, perm[a]]) / (math.pi / 2))) % 4
                        acc = times_i(power, *terms[a]) if acc is None else add_times_i(power, acc, terms[a])
                    for re_im in range(2):
                        start = pl.multiple_of((re_im * 32 + n * 16 + g) * 8, 8)
                        cur[pl.ds(start, 8), :] = acc[re_im]
            return carry

        lax.fori_loop(0, 2, gammas, 0)
        out = jnp.zeros((32, 128), jnp.float32)
        contract = (((1,), (1,)), ((), ()))
        for s in range(8):
            both = jnp.concatenate([cur[pl.ds(s, 32, stride=8), :], cur[pl.ds(256 + s, 32, stride=8), :]], axis=1)
            hi = both.astype(jnp.bfloat16)
            lo = (both - hi.astype(jnp.float32)).astype(jnp.bfloat16)
            wide = slice(s * 256, s * 256 + 256)
            ph, plo = phase_hi[:, wide], phase_lo[:, wide]
            main = lax.dot_general(jnp.concatenate([hi, lo], axis=0), ph, contract, preferred_element_type=jnp.float32)
            out = out + main[:32] + main[32:]
            out = out + lax.dot_general(hi, plo, contract, preferred_element_type=jnp.float32)
        loop_s[pl.ds(q, 32, stride=8), :] = out

    def loops_send():
        def step(d, carry):
            target = lax.rem(x + d, n_space)
            pltpu.make_async_remote_copy(
                src_ref=loop_s.at[pl.ds(pl.multiple_of(target * 8, 8), 8)], dst_ref=loop_r.at[n_space - 1 - d],
                send_sem=loop_ssem, recv_sem=loop_rsem, device_id=(target, t), device_id_type=MESH,
            ).start()
            return carry

        lax.fori_loop(1, n_space, step, 0)

    def nothing():
        pass

    zero = jnp.zeros((4, 3, 8, 128), jnp.float32)
    field[5, 0] = zero
    field[5, 1] = zero
    cr, ci = clover_apply(wclov.at[1, 1], sfield[1, 0], sfield[1, 1])
    inner[4, 0] = cr
    inner[4, 1] = ci
    hr, hi = hop(0, 1, cr, ci, nothing, nothing)
    field[0, 0] = sfield[0, 0] + KAPPA * hr
    field[0, 1] = sfield[0, 1] + KAPPA * hi

    def pair(p, carry):
        forward = p % 2
        g5 = (2 * forward - 1).astype(jnp.float32)
        later = p > 0

        def flip(v):
            return jnp.concatenate([v[:2], v[2:] * g5], axis=0)

        def early_a():
            @pl.when(later)
            def _():
                norm_send_a(p - 1)

        def late_b():
            @pl.when(later)
            def _():
                q = p - 1
                project_loops(q, jnp.where(q == 0, 5, 2 * q - 1), jnp.where(q == 0, 4, 2 * q - 1))

            @pl.when(p == 3)
            def _():
                loops_send()

        def early_b():
            @pl.when(later)
            def _():
                norm_recv_a(p - 1)
                norm_send_b(p - 1)

        fr, fi = field[p, 0], field[p, 1]
        hr, hi = hop(2 * p + 1, 0, flip(fr), flip(fi), early_a, nothing)
        vr, vi = clover_apply(wclov.at[forward, 1], hr, hi)
        vr, vi = KAPPA * vr, KAPPA * vi
        inner[p, 0] = vr
        inner[p, 1] = vi
        hr, hi = hop(2 * p + 2, 1, vr, vi, early_b, late_b)
        cr, ci = clover_apply(wclov.at[forward, 0], field[p, 0], field[p, 1])
        outr, outi = cr - KAPPA * flip(hr), ci - KAPPA * flip(hi)
        field[p + 1, 0] = outr
        field[p + 1, 1] = outi

        @pl.when(later)
        def _():
            norm_recv_b(p - 1)

        @pl.when(p == 2)
        def _():
            rr, image = total(0), total(1)
            alpha = spread([rr[n] / image[n] for n in range(2)])
            for re_im in range(2):
                field[3, re_im] = field[1, re_im] - alpha * field[3, re_im]

        @pl.when(p == 3)
        def _():
            new, rr = total(2), total(0)
            beta = spread([new[n] / rr[n] for n in range(2)])
            for re_im in range(2):
                field[4, re_im] = field[4, re_im] + beta * field[2, re_im]

        norm_local(p, field[p + 1, 0], field[p + 1, 1])
        return carry

    lax.fori_loop(0, 4, pair, 0)

    norm_send_a(3)
    norm_recv_a(3)
    norm_send_b(3)
    pltpu.make_async_copy(loop_r, loop_r, loop_rsem).wait()
    own = loop_s[pl.ds(pl.multiple_of(x * 8, 8), 8), :]
    piece = own + jnp.sum(loop_r[...], axis=0)
    second = x >= n_space // 2
    angle = momrow[0:1, :].astype(jnp.int32) * second.astype(jnp.int32)
    cos, sin = cos_sin(angle & 31)
    sin = jnp.where(lane1 < 64, -sin, sin)
    norm_recv_b(3)

    rr0, im0, rr1, im1 = [jnp.where(second, pair_[1], pair_[0]) for pair_ in (total(0), total(1), total(2), total(3))]
    alpha0, alpha1, beta = rr0 / im0, rr1 / im1, rr1 / rr0
    line = piece[0:1] + (alpha0 + alpha1 * beta) * piece[1:2] + alpha1 * piece[2:3]
    line = (line * cos + pltpu.roll(line, 64, 1) * sin) * (1.0 / math.sqrt(n_space * NY * NZ))
    out_ref[0] = line[:, 0:n_mom]
    out_ref[1] = line[:, 64 : 64 + n_mom]

    pltpu.make_async_copy(send, send, send_sem).wait()
    for p in range(4):
        for stage, ref in enumerate((norm_ar, norm_br)):
            pltpu.make_async_copy(ref.at[p], ref.at[p], norm_ssem.at[p, stage]).wait()
    pltpu.make_async_copy(loop_r, loop_r, loop_ssem).wait()


def solution(mesh):
    n_space, n_tm = mesh.shape["space"], mesh.shape["tm"]

    def local(sources, links, clover, momenta):
        f32 = jnp.float32
        n_mom = momenta.shape[0]
        tile = (8, 128)
        scratch = [
            pltpu.VMEM((2, 2, 4, 3) + tile, f32),
            pltpu.VMEM((4, 2, 3, 3) + tile, f32),
            pltpu.VMEM((2, 2, 6, 6) + tile, f32),
            pltpu.VMEM((2, 4, 2, 3, 3) + tile, f32),
            pltpu.VMEM((2, 2, 2, 2, 6, 6) + tile, f32),
            pltpu.VMEM((2, 2, 4, 3) + tile, f32),
            pltpu.VMEM((6, 2, 4, 3) + tile, f32),
            pltpu.VMEM((5, 2, 4, 3) + tile, f32),
            pltpu.VMEM((2, 2, 4, 4) + tile, f32),
            pltpu.VMEM((512, 128), f32),
            pltpu.VMEM((128, 2048), jnp.bfloat16),
            pltpu.VMEM((128, 2048), jnp.bfloat16),
            pltpu.VMEM(tile, f32),
            pltpu.VMEM((9, 4, 2, 2, 3) + tile, f32),
            pltpu.VMEM((9, 4, 2, 2, 3) + tile, f32),
            pltpu.VMEM((4,) + tile, f32),
            pltpu.VMEM((4, n_tm - 1) + tile, f32),
            pltpu.VMEM((4,) + tile, f32),
            pltpu.VMEM((4, n_space - 1) + tile, f32),
            pltpu.VMEM((4,) + tile, f32),
            pltpu.VMEM((256, 128), f32),
            pltpu.VMEM((n_space - 1,) + tile, f32),
            pltpu.SemaphoreType.DMA((3,)),
            pltpu.SemaphoreType.DMA,
            pltpu.SemaphoreType.DMA((9, 4)),
            pltpu.SemaphoreType.DMA((4, 2)),
            pltpu.SemaphoreType.DMA((4, 2)),
            pltpu.SemaphoreType.DMA,
            pltpu.SemaphoreType.DMA,
        ]
        out = pl.pallas_call(
            lambda *refs: kernel(n_space, n_tm, *refs),
            out_shape=jax.ShapeDtypeStruct((2, 1, n_mom), f32),
            in_specs=[pl.BlockSpec(memory_space=pl.ANY)] * 3 + [pl.BlockSpec(memory_space=pltpu.VMEM)],
            out_specs=pl.BlockSpec(memory_space=pltpu.VMEM),
            scratch_shapes=scratch,
            compiler_params=pltpu.CompilerParams(
                collective_id=0, has_side_effects=True, vmem_limit_bytes=32 * 1024 * 1024
            ),
            name="loops",
        )(
            sources.reshape((2, 2, 4, 3) + tile),
            links.reshape((4, 2, 3, 3) + tile),
            clover.reshape((2, 2, 6, 6) + tile),
            momenta.T,
        )
        return out.reshape(2, 1, n_mom, 1)

    placed = P(None, None, None, None, "space", "tm", None)
    return jax.shard_map(
        local, mesh=mesh, in_specs=(placed, placed, placed, P()), out_specs=P(None, "space", None, "tm"), check_vma=False
    )
```

profile of v0, /device:TPU:1, one launch (start us, length us, event | category | flops | bytes accessed | tf_op | source)
XLA Modules:
  0.0 65.9 jit_solution(10448102186134930007)
XLA Ops:
  0.0 0.0 copy-start.3
  0.0 0.7 %copy-done.3 = s32[33,3]{0,1:T(4,128)S(1)} copy-done((s32[33,3]{0,1:T(4,128)S(1)}, s32[33,3]{0,1:T(4,128)}, u32[]{:S(2)}) %copy-start.3) | copy-done | bytes 420
  0.7 0.0 copy-start
  0.7 1.1 %copy-done = f32[2,2,6,6,1,1,1024]{6,5,4,3,2,1,0:T(1,128)S(1)} copy-done((f32[2,2,6,6,1,1,1024]{6,5,4,3,2,1,0:T(1,128)S(1)}, f32[2,2,6,6,1,1,1024]{6,5,4,3,2,1,0:T(1,128)}, u32[]{:S(2)}) %copy-start) | copy-done | bytes 589848
  1.7 0.0 copy-start.1
  1.7 1.0 %copy-done.1 = f32[4,2,3,3,1,1,1024]{6,5,4,3,2,1,0:T(1,128)S(1)} copy-done((f32[4,2,3,3,1,1,1024]{6,5,4,3,2,1,0:T(1,128)S(1)}, f32[4,2,3,3,1,1,1024]{6,5,4,3,2,1,0:T(1,128)}, u32[]{:S(2)}) %copy-start.1) | copy-done | bytes 294936
  2.7 0.0 copy-start.2
  2.7 0.9 %copy-done.2 = f32[2,2,4,3,1,1,1024]{6,5,4,3,2,1,0:T(1,128)S(1)} copy-done((f32[2,2,4,3,1,1,1024]{6,5,4,3,2,1,0:T(1,128)S(1)}, f32[2,2,4,3,1,1,1024]{6,5,4,3,2,1,0:T(1,128)}, u32[]{:S(2)}) %copy-start.2) | copy-done | bytes 196632
  3.6 61.7 %loops.1 = f32[2,1,33]{2,1,0:T(1,128)S(1)} custom-call(f32[2,2,4,3,8,128]{5,4,3,2,1,0:T(8,128)S(1)} %bitcast.9, f32[4,2,3,3,8,128]{5,4,3,2,1,0:T(8,128)S(1)} %bitcast.8, f32[2,2,6,6,8,128]{5,4,3,2,1,0:T(8,128)S(1)} %bitcast.7, s32[3,33]{1,0:T(4,128)S(1)} %bitcast.11), custom_call_target="tpu_custom_call" | custom-call | tf_op jit(solution)/shard_map/loops/pallas_call | solution.py:521
  65.3 0.6 copy.7
Async XLA Ops:
  0.0 0.7 %copy-start.3 = (s32[33,3]{0,1:T(4,128)S(1)}, s32[33,3]{0,1:T(4,128)}, u32[]{:S(2)}) copy-start(s32[33,3]{0,1:T(4,128)} %param.7) | copy-start | bytes 1192
  0.7 1.1 %copy-start = (f32[2,2,6,6,1,1,1024]{6,5,4,3,2,1,0:T(1,128)S(1)}, f32[2,2,6,6,1,1,1024]{6,5,4,3,2,1,0:T(1,128)}, u32[]{:S(2)}) copy-start(f32[2,2,6,6,1,1,1024]{6,5,4,3,2,1,0:T(1,128)} %param.6) | copy-start | bytes 1769476
  1.7 1.0 %copy-start.1 = (f32[4,2,3,3,1,1,1024]{6,5,4,3,2,1,0:T(1,128)S(1)}, f32[4,2,3,3,1,1,1024]{6,5,4,3,2,1,0:T(1,128)}, u32[]{:S(2)}) copy-start(f32[4,2,3,3,1,1,1024]{6,5,4,3,2,1,0:T(1,128)} %param.5) | copy-start | bytes 884740
  2.7 0.9 %copy-start.2 = (f32[2,2,4,3,1,1,1024]{6,5,4,3,2,1,0:T(1,128)S(1)}, f32[2,2,4,3,1,1,1024]{6,5,4,3,2,1,0:T(1,128)}, u32[]{:S(2)}) copy-start(f32[2,2,4,3,1,1,1024]{6,5,4,3,2,1,0:T(1,128)} %param.4) | copy-start | bytes 589828
where the time goes:
time: 66.1 us; the launch traced here: 65.9 us
  Pallas kernels  61.7 us (93%)
  local copies, waits for them, and re-layouts  4.2 us (6%)
    pallas_call x1, Pallas kernels, local(): pl.pallas_call(lambda *refs: kernel(n_space, n_tm, *refs), out_shape=jax....  61.7 us
    unnamed x9, local copies, waits for them, and re-layouts  4.2 us

commit v1 on v0

v1 whole, which is shorter than its diff:
```python
import math

import jax
import jax.numpy as jnp
import numpy as np
from jax import lax
from jax.experimental import pallas as pl
from jax.experimental.pallas import tpu as pltpu
from jax.sharding import PartitionSpec as P

MESH = pl.DeviceIdType.MESH
NZ = 32
NY = 32
KAPPA = 0.1
MOM = 48
UNROLL = True


UPPER = (((1, 1), (0, 1)), ((1, 0), (0, 2)), ((0, 1), (1, 3)), ((0, 0), (1, 0)))
LOWER = (((1, 3), (0, 3)), ((1, 2), (0, 0)), ((0, 3), (1, 1)), ((0, 0), (1, 0)))


def gamma_products():
    sigma = [
        np.array([[0, 1], [1, 0]]) + 0j,
        np.array([[0, -1j], [1j, 0]]),
        np.array([[1, 0], [0, -1]]) + 0j,
    ]
    zero = np.zeros((2, 2)) + 0j
    singles = [np.block([[zero, 1j * s], [-1j * s, zero]]) for s in sigma]
    singles.append(np.block([[zero, np.eye(2)], [np.eye(2), zero]]) + 0j)
    products = []
    for bits in range(16):
        product = np.eye(4) + 0j
        for direction in range(4):
            if bits >> direction & 1:
                product = product @ singles[direction]
        products.append(product)
    return products


def times_i(power, re, im):
    power %= 4
    if power == 0:
        return re, im
    if power == 1:
        return -im, re
    if power == 2:
        return -re, -im
    return im, -re


def add_times_i(power, acc, term):
    (ar, ai), (re, im) = acc, term
    power %= 4
    if power == 0:
        return ar + re, ai + im
    if power == 1:
        return ar - im, ai + re
    if power == 2:
        return ar - re, ai - im
    return ar + im, ai - re


def color_apply(link, half, adjoint):
    hr, hi = half
    outr = outi = None
    for b in range(3):
        if adjoint:
            ur, ui = link[0, b], link[1, b]
        else:
            ur, ui = link[0, :, b], link[1, :, b]
        ur, ui = ur[None], ui[None]
        xr, xi = hr[:, b][:, None], hi[:, b][:, None]
        if adjoint:
            tr, ti = ur * xr + ui * xi, ur * xi - ui * xr
        else:
            tr, ti = ur * xr - ui * xi, ur * xi + ui * xr
        outr, outi = (tr, ti) if outr is None else (outr + tr, outi + ti)
    return outr, outi


def clover_apply(mat, fr, fi):
    xr, xi = fr.reshape(2, 6, 8, 128), fi.reshape(2, 6, 8, 128)
    outr = outi = None
    for i in range(6):
        cr, ci = mat[0, :, :, i], mat[1, :, :, i]
        vr, vi = xr[:, i][:, None], xi[:, i][:, None]
        tr, ti = cr * vr - ci * vi, cr * vi + ci * vr
        outr, outi = (tr, ti) if outr is None else (outr + tr, outi + ti)
    return outr.reshape(4, 3, 8, 128), outi.reshape(4, 3, 8, 128)


def fan(ys, xs, cores, zs):
    offsets = [(y, x, c, z) for y in ys for x in xs for c in cores for z in zs if (y, x, c, z) != (0, 0, 0, 0)]
    return sorted(offsets, key=lambda o: -(min(o[0], 4 - o[0]) + min(o[1], 4 - o[1]) + min(o[3], 4 - o[3])))


ALONG_ROW = fan([0], range(4), range(2), [0])
ALONG_Y = fan(range(4), [0], [0], [0])
ALONG_Z = fan([0], [0], [0], range(4))
ALONG_SPACE = fan(range(4), range(4), range(2), [0])
ROUNDS = (ALONG_ROW, ALONG_Y, ALONG_Z)


def when(condition):
    if isinstance(condition, bool):
        return (lambda f: f()) if condition else (lambda f: None)
    return pl.when(condition)


def pick(condition, a, b):
    if isinstance(condition, bool):
        return a if condition else b
    return jnp.where(condition, a, b)


def kernel(
    n_space, n_tm,
    src_hbm, clov_hbm, link_hbm, mom_hbm, out_ref,
    src, clov, link, mom_ref, wlink, wclov, sfield, field, inner, base, bil, cur, phase_hi, phase_lo, momrow,
    send, recv, row_s, row_r0, row_r1, row_r2, last_r1, last_r2, alpha_ref, loop_s, loop_r,
    in_sem, send_sem, recv_sem, row_ssem, row_rsem, loop_ssem, loop_rsem,
):
    x = lax.axis_index("space")
    t = lax.axis_index("tm")
    x_up, x_dn = lax.rem(x + 1, n_space), lax.rem(x + n_space - 1, n_space)
    t_up, t_dn = lax.rem(t + 1, n_tm), lax.rem(t + n_tm - 1, n_tm)

    loads = [
        pltpu.make_async_copy(a, b, in_sem.at[k])
        for k, (a, b) in enumerate(((src_hbm, src), (clov_hbm, clov), (link_hbm, link), (mom_hbm, mom_ref)))
    ]
    for load in loads:
        load.start()

    def space_at(dy, dx, dc):
        return ((x // 8 + dy) & 3) * 8 + (((x // 2) + dx) & 3) * 2 + ((x + dc) & 1)

    def place(offset):
        dy, dx, dc, dz = offset
        return (space_at(dy, dx, dc), (t + dz) & 3)

    barrier = pltpu.get_barrier_semaphore()
    greeted = ALONG_SPACE + ALONG_Z
    for offset in greeted:
        pl.semaphore_signal(barrier, inc=1, device_id=place(offset), device_id_type=MESH)

    lane = lax.broadcasted_iota(jnp.int32, (8, 128), 1)
    row = lax.broadcasted_iota(jnp.int32, (8, 128), 0)
    lane1 = lax.broadcasted_iota(jnp.int32, (1, 128), 1)
    zc = lane & 31
    yc = row * 4 + (lane >> 5)
    ev = ((yc + zc + x + t) & 1) == 0

    def move(v, axis, by):
        last = v.ndim - 1
        if axis == 2:
            if by == 1:
                return jnp.where(zc == 31, pltpu.roll(v, 31, last), pltpu.roll(v, 127, last))
            return jnp.where(zc == 0, pltpu.roll(v, 97, last), pltpu.roll(v, 1, last))
        if by == 1:
            a = pltpu.roll(v, 96, last)
            return jnp.where(lane >= 96, pltpu.roll(a, 7, last - 1), a)
        a = pltpu.roll(v, 32, last)
        return jnp.where(lane < 32, pltpu.roll(a, 1, last - 1), a)

    def cos_sin(k):
        a = (k - 16).astype(jnp.float32) * (math.pi / 32)
        q = a * a
        s = 1.0 / math.factorial(11)
        for m in (9, 7, 5, 3, 1):
            s = 1.0 / math.factorial(m) - q * s
        s = s * a
        c = 1.0 / math.factorial(12)
        for m in (10, 8, 6, 4, 2, 0):
            c = 1.0 / math.factorial(m) - q * c
        return 2.0 * s * s - 1.0, -2.0 * s * c

    def pack_clover(entries):
        def step(k, carry):
            re_im, chi, r = k // 12, (k // 6) % 2, k % 6
            sign = (1 - 2 * re_im).astype(jnp.float32)
            a = clov[re_im, chi, r]
            b = move(a, 2, -1)
            for forward, par in entries:
                v = jnp.where(ev, a, b) if par == 0 else jnp.where(ev, b, a)
                if forward:
                    wclov[1, par, re_im, chi, r] = v
                else:
                    wclov[0, par, re_im, chi, :, r] = v * sign
            return carry

        lax.fori_loop(0, 24, step, 0)

    t_sign = jnp.where(t == n_tm - 1, -1.0, 1.0).astype(jnp.float32)

    def pack_links(directions):
        for mu in directions:
            for re_im in range(2):
                a = link[mu, re_im]
                if mu == 3:
                    a = a * t_sign
                b = move(a, 2, -1)
                wlink[0, mu, re_im] = jnp.where(ev, a, b)
                wlink[1, mu, re_im] = jnp.where(ev, b, a)

    n_mom = mom_ref.shape[1]

    def make_phases():
        loads[3].wait()
        mom = mom_ref[...].astype(jnp.float32)
        eye = lax.broadcasted_iota(jnp.int32, (MOM, n_mom), 0) == lax.broadcasted_iota(jnp.int32, (MOM, n_mom), 1)
        columns = [
            jnp.sum(jnp.where(eye, jnp.broadcast_to(mom[k : k + 1], (MOM, n_mom)), 0.0), axis=1, keepdims=True).astype(jnp.int32)
            for k in range(3)
        ]
        zero_rows = jnp.zeros((64 - MOM, 2048), jnp.bfloat16)
        for ref in (phase_hi, phase_lo):
            ref[MOM:64, :] = zero_rows
            ref[64 + MOM : 128, :] = zero_rows

        def phases(s, carry):
            yrow = s * 4 + (lane1 >> 5)
            zrow = lane1 & 31
            c, sn = cos_sin((columns[0] * x + columns[1] * yrow + columns[2] * zrow) & 31)
            for value, places in ((c, ((0, 0, 1), (64, 128, 1))), (sn, ((0, 128, 1), (64, 0, -1)))):
                hi = value.astype(jnp.bfloat16)
                lo = (value - hi.astype(jnp.float32)).astype(jnp.bfloat16)
                for r0, c0, sign in places:
                    at = pl.ds(pl.multiple_of(s * 256 + c0, 128), 128)
                    phase_hi[r0 : r0 + MOM, at] = hi * sign
                    phase_lo[r0 : r0 + MOM, at] = lo * sign
            return carry

        lax.fori_loop(0, 8, phases, 0)
        momrow[...] = jnp.zeros_like(momrow)
        momrow[0:1, 0:n_mom] = mom[2:3]
        momrow[0:1, 64 : 64 + n_mom] = mom[2:3]
        loop_s[...] = jnp.zeros_like(loop_s)
        zero = jnp.zeros((4, 3, 8, 128), jnp.float32)
        field[5, 0] = zero
        field[5, 1] = zero

    ROUTES = ((0, -1, (x_dn, t)), (0, 1, (x_up, t)), (3, -1, (x, t_dn)), (3, 1, (x, t_up)))

    def halo(j, k):
        return pltpu.make_async_remote_copy(
            src_ref=send.at[j, k], dst_ref=recv.at[j, k], send_sem=send_sem, recv_sem=recv_sem.at[j, k],
            device_id=ROUTES[k][2], device_id_type=MESH,
        )

    def project(fr, fi, mu, sign):
        rows_r, rows_i = [], []
        for spin in range(2):
            col, power = UPPER[mu][spin]
            if sign < 0:
                power += 2
            r, i = add_times_i(power, (fr[spin], fi[spin]), (fr[2 + col], fi[2 + col]))
            rows_r.append(r)
            rows_i.append(i)
        return jnp.stack(rows_r), jnp.stack(rows_i)

    def add_up(acc, half, mu, sign):
        hr, hi = half
        for spin in range(2):
            acc[spin] = (hr[spin], hi[spin]) if acc[spin] is None else (acc[spin][0] + hr[spin], acc[spin][1] + hi[spin])
            col, power = LOWER[mu][spin]
            if sign < 0:
                power += 2
            term = (hr[col], hi[col])
            acc[2 + spin] = times_i(power, *term) if acc[2 + spin] is None else add_times_i(power, acc[2 + spin], term)

    def hop(j, par, fr, fi, early, late):
        to = 1 - par
        for k, (mu, sign, _) in enumerate(ROUTES):
            half = project(fr, fi, mu, sign)
            if sign > 0:
                half = color_apply(wlink.at[par, mu], half, True)
            send[j, k, 0] = half[0]
            send[j, k, 1] = half[1]
            halo(j, k).start()
        early()
        acc = [None] * 4
        for mu in (1, 2):
            hr, hi = project(fr, fi, mu, -1)
            ahead = (move(hr, mu, 1), move(hi, mu, 1))
            add_up(acc, color_apply(wlink.at[to, mu], ahead, False), mu, -1)
            hr, hi = color_apply(wlink.at[par, mu], project(fr, fi, mu, 1), True)
            add_up(acc, (move(hr, mu, -1), move(hi, mu, -1)), mu, 1)
        late()
        for k in (2, 3, 0, 1):
            mu, sign, _ = ROUTES[k]
            halo(j, k).wait_recv()
            half = (recv[j, k, 0], recv[j, k, 1])
            if sign < 0:
                half = color_apply(wlink.at[to, mu], half, False)
            add_up(acc, half, mu, sign)
        return jnp.stack([a[0] for a in acc]), jnp.stack([a[1] for a in acc])

    def to_row(tiles):
        out = jnp.zeros((8, 128), jnp.float32)
        for k, tile in enumerate(tiles):
            for n in range(2):
                part = jnp.where(ev, tile, 0.0) if n == 0 else jnp.where(ev, 0.0, tile)
                out = jnp.where(row == 2 * k + n, jnp.sum(part, axis=0, keepdims=True), out)
        for by in (64, 32, 16):
            out = out + pltpu.roll(out, by, 1)
        return jnp.sum(jnp.where(lane >> 4 == row, out, 0.0), axis=0, keepdims=True)

    def from_row(line, k):
        return [
            jnp.sum(jnp.where(lane1 >> 4 == 2 * k + n, line, 0.0), axis=1, keepdims=True) for n in range(2)
        ]

    def row_send(group, slot, dst, stage):
        for k, offset in enumerate(group):
            pltpu.make_async_remote_copy(
                src_ref=row_s.at[slot, pl.ds(0, 1)], dst_ref=dst.at[pl.ds(k, 1)], send_sem=row_ssem.at[stage],
                recv_sem=row_rsem.at[stage], device_id=place(offset), device_id_type=MESH,
            ).start()

    def row_recv(slot, dst, stage):
        pltpu.make_async_copy(dst, dst, row_rsem.at[stage]).wait()
        return row_s[slot, 0:1, :] + jnp.sum(dst[...], axis=0, keepdims=True)

    first_r = (row_r0, row_r1, row_r2)

    def spread(pair):
        return jnp.where(ev, jnp.broadcast_to(pair[0], (8, 128)), jnp.broadcast_to(pair[1], (8, 128)))

    products = gamma_products()

    def project_loops(q, at_field, at_inner):
        for a in range(4):
            par_r, par_i = [], []
            for par, ref, at in ((0, field, at_field), (1, inner, at_inner)):
                br = bi = None
                for c in range(3):
                    sr, si = sfield[par, 0, a, c], sfield[par, 1, a, c]
                    pr, pi = ref[at, 0, :, c], ref[at, 1, :, c]
                    tr, ti = sr * pr + si * pi, sr * pi - si * pr
                    br, bi = (tr, ti) if br is None else (br + tr, bi + ti)
                par_r.append(br)
                par_i.append(bi)
            for re_im, (e, o) in enumerate((par_r, par_i)):
                bil[0, re_im, a] = jnp.where(ev, e, o)
                bil[1, re_im, a] = jnp.where(ev, o, e)

        def gammas(n, carry):
            for first in range(4):
                group = [g for g in range(16) if abs(products[g][0, first]) > 0.5]
                perm = [int(np.argmax(np.abs(products[group[0]][a]))) for a in range(4)]
                terms = [(bil[n, 0, a, perm[a]], bil[n, 1, a, perm[a]]) for a in range(4)]
                for g in group:
                    acc = None
                    for a in range(4):
                        power = int(round(np.angle(products[g][a, perm[a]]) / (math.pi / 2))) % 4
                        acc = times_i(power, *terms[a]) if acc is None else add_times_i(power, acc, terms[a])
                    for re_im in range(2):
                        start = pl.multiple_of((re_im * 32 + n * 16 + g) * 8, 8)
                        cur[pl.ds(start, 8), :] = acc[re_im]
            return carry

        lax.fori_loop(0, 2, gammas, 0)
        out = jnp.zeros((32, 128), jnp.float32)
        contract = (((1,), (1,)), ((), ()))
        for s in range(8):
            both = jnp.concatenate([cur[pl.ds(s, 32, stride=8), :], cur[pl.ds(256 + s, 32, stride=8), :]], axis=1)
            hi = both.astype(jnp.bfloat16)
            lo = (both - hi.astype(jnp.float32)).astype(jnp.bfloat16)
            wide = slice(s * 256, s * 256 + 256)
            ph, plo = phase_hi[:, wide], phase_lo[:, wide]
            main = lax.dot_general(jnp.concatenate([hi, lo], axis=0), ph, contract, preferred_element_type=jnp.float32)
            out = out + main[:32] + main[32:]
            out = out + lax.dot_general(hi, plo, contract, preferred_element_type=jnp.float32)
        loop_s[pl.ds(q, 32, stride=8), :] = out

    def loops_send():
        for k, offset in enumerate(ALONG_SPACE):
            target, _ = place(offset)
            pltpu.make_async_remote_copy(
                src_ref=loop_s.at[pl.ds(pl.multiple_of(target * 8, 8), 8)], dst_ref=loop_r.at[k],
                send_sem=loop_ssem, recv_sem=loop_rsem, device_id=(target, t), device_id_type=MESH,
            ).start()

    def nothing():
        pass

    def pair(p, carry):
        forward = p % 2
        g5 = 2.0 * forward - 1.0 if isinstance(p, int) else (2 * forward - 1).astype(jnp.float32)

        def flip(v):
            return jnp.concatenate([v[:2], v[2:] * g5], axis=0)

        def early_a():
            @when(p == 2)
            def _():
                row_send(ROUNDS[0], 0, first_r[0], 0)

            @when(p == 3)
            def _():
                row_send(ROUNDS[2], 2, first_r[2], 2)

        def late_a():
            @when(p == 0)
            def _():
                make_phases()

        def early_b():
            @when(p == 2)
            def _():
                row_s[1, 0:1, :] = row_recv(0, first_r[0], 0)
                row_send(ROUNDS[1], 1, first_r[1], 1)

        def late_b():
            cr, ci = clover_apply(wclov.at[forward, 0], field[p, 0], field[p, 1])
            base[0] = cr
            base[1] = ci

            @when(p == 3)
            def _():
                line = row_recv(2, first_r[2], 2)
                row_s[3, 0:1, :] = line
                rr, image = from_row(line, 0), from_row(line, 1)
                alpha = spread([rr[n] / image[n] for n in range(2)])
                alpha_ref[0] = alpha
                alpha_odd = spread([rr[1 - n] / image[1 - n] for n in range(2)])
                sq = None
                for re_im in range(2):
                    r = field[1, re_im] - alpha * field[3, re_im]
                    field[6, re_im] = r
                    inner[5, re_im] = inner[1, re_im] - alpha_odd * inner[3, re_im]
                    s = jnp.sum(r * r, axis=(0, 1))
                    sq = s if sq is None else sq + s
                alpha_ref[1] = sq

            @when(p > 0)
            def _():
                at_field = pick(p == 1, 5, pick(p == 2, 1, 6))
                at_inner = pick(p == 1, 4, pick(p == 2, 1, 5))
                project_loops(p - 1, at_field, at_inner)

            @when(p == 3)
            def _():
                loops_send()

        fr, fi = field[p, 0], field[p, 1]
        hr, hi = hop(2 * p + 1, 0, flip(fr), flip(fi), early_a, late_a)
        vr, vi = clover_apply(wclov.at[forward, 1], hr, hi)
        vr, vi = KAPPA * vr, KAPPA * vi
        inner[p, 0] = vr
        inner[p, 1] = vi
        hr, hi = hop(2 * p + 2, 1, vr, vi, early_b, late_b)
        outr, outi = base[0] - KAPPA * flip(hr), base[1] - KAPPA * flip(hi)
        field[p + 1, 0] = outr
        field[p + 1, 1] = outi

        @when(p == 1)
        def _():
            r0, r1 = field[1, 0], field[1, 1]
            i0, i1 = field[2, 0], field[2, 1]
            tiles = [jnp.sum(a * a + b * b, axis=(0, 1)) for a, b in ((r0, r1), (i0, i1))]
            row_s[0, 0:1, :] = to_row(tiles)

        @when(p == 2)
        def _():
            row_s[2, 0:1, :] = row_recv(1, first_r[1], 1)

        return carry

    loads[0].wait()
    for re_im in range(2):
        a = src[0, re_im]
        b = move(src[1, re_im], 2, -1)
        sfield[0, re_im] = jnp.where(ev, a, b)
        sfield[1, re_im] = jnp.where(ev, b, a)
    loads[1].wait()
    pack_clover(((1, 1),))
    cr, ci = clover_apply(wclov.at[1, 1], sfield[1, 0], sfield[1, 1])
    inner[4, 0] = cr
    inner[4, 1] = ci
    loads[2].wait()
    pack_links((0, 3))
    pl.semaphore_wait(barrier, len(greeted))
    hr, hi = hop(
        0, 1, cr, ci, lambda: pack_links((1, 2)), lambda: pack_clover(((0, 1), (0, 0), (1, 0)))
    )
    field[0, 0] = sfield[0, 0] + KAPPA * hr
    field[0, 1] = sfield[0, 1] + KAPPA * hi

    if UNROLL:
        for p in range(4):
            pair(p, 0)
    else:
        lax.fori_loop(0, 4, pair, 0)

    alpha = alpha_ref[0]
    m1 = m2 = None
    for re_im in range(2):
        v, w = field[2, re_im] - alpha * field[4, re_im], field[2, re_im]
        a, b = jnp.sum(v * v, axis=(0, 1)), jnp.sum(v * w, axis=(0, 1))
        m1, m2 = (a, b) if m1 is None else (m1 + a, m2 + b)
    row_s[4, 0:1, :] = to_row([alpha_ref[1], m1, m2])
    row_send(ALONG_Z, 4, last_r1, 3)
    second = x >= n_space // 2
    angle = momrow[0:1, :].astype(jnp.int32) * second.astype(jnp.int32)
    cos, sin = cos_sin(angle & 31)
    sin = jnp.where(lane1 < 64, -sin, sin)
    row_s[5, 0:1, :] = row_recv(4, last_r1, 3)
    row_send(ALONG_SPACE, 5, last_r2, 4)
    pltpu.make_async_copy(loop_r, loop_r, loop_rsem).wait()
    own = loop_s[pl.ds(pl.multiple_of(x * 8, 8), 8), :]
    piece = own + jnp.sum(loop_r[...], axis=0)
    piece = piece * cos + pltpu.roll(piece, 64, 1) * sin
    piece = piece * (1.0 / math.sqrt(n_space * NY * NZ))
    start = row_s[3, 0:1, :]
    rr0, im0 = [jnp.where(second, v[1], v[0]) for v in (from_row(start, 0), from_row(start, 1))]
    line = row_recv(5, last_r2, 4)
    rr1, m1, m2 = [jnp.where(second, v[1], v[0]) for v in (from_row(line, 0), from_row(line, 1), from_row(line, 2))]
    alpha0, beta = rr0 / im0, rr1 / rr0
    alpha1 = rr1 / (m1 + beta * (2.0 * m2 + beta * im0))
    line = piece[0:1] + (alpha0 + alpha1 * beta) * piece[1:2] + alpha1 * piece[2:3]
    out_ref[0] = line[:, 0:n_mom]
    out_ref[1] = line[:, 64 : 64 + n_mom]

    pltpu.make_async_copy(send, send, send_sem).wait()
    for stage, ref in enumerate((row_r0, row_r1, row_r2, last_r1, last_r2)):
        pltpu.make_async_copy(ref, ref, row_ssem.at[stage]).wait()
    pltpu.make_async_copy(loop_r, loop_r, loop_ssem).wait()


def solution(mesh):
    n_space, n_tm = mesh.shape["space"], mesh.shape["tm"]

    def local(sources, links, clover, momenta):
        f32 = jnp.float32
        n_mom = momenta.shape[0]
        tile = (8, 128)
        scratch = [
            pltpu.VMEM((2, 2, 4, 3) + tile, f32),
            pltpu.VMEM((2, 2, 6, 6) + tile, f32),
            pltpu.VMEM((4, 2, 3, 3) + tile, f32),
            pltpu.VMEM((3, n_mom), jnp.int32),
            pltpu.VMEM((2, 4, 2, 3, 3) + tile, f32),
            pltpu.VMEM((2, 2, 2, 2, 6, 6) + tile, f32),
            pltpu.VMEM((2, 2, 4, 3) + tile, f32),
            pltpu.VMEM((7, 2, 4, 3) + tile, f32),
            pltpu.VMEM((6, 2, 4, 3) + tile, f32),
            pltpu.VMEM((2, 4, 3) + tile, f32),
            pltpu.VMEM((2, 2, 4, 4) + tile, f32),
            pltpu.VMEM((512, 128), f32),
            pltpu.VMEM((128, 2048), jnp.bfloat16),
            pltpu.VMEM((128, 2048), jnp.bfloat16),
            pltpu.VMEM(tile, f32),
            pltpu.VMEM((9, 4, 2, 2, 3) + tile, f32),
            pltpu.VMEM((9, 4, 2, 2, 3) + tile, f32),
            pltpu.VMEM((6,) + tile, f32),
            *[pltpu.VMEM((len(group), 128), f32) for group in ROUNDS + (ALONG_Z, ALONG_SPACE)],
            pltpu.VMEM((2,) + tile, f32),
            pltpu.VMEM((256, 128), f32),
            pltpu.VMEM((n_space - 1,) + tile, f32),
            pltpu.SemaphoreType.DMA((4,)),
            pltpu.SemaphoreType.DMA,
            pltpu.SemaphoreType.DMA((9, 4)),
            pltpu.SemaphoreType.DMA((5,)),
            pltpu.SemaphoreType.DMA((5,)),
            pltpu.SemaphoreType.DMA,
            pltpu.SemaphoreType.DMA,
        ]
        out = pl.pallas_call(
            lambda *refs: kernel(n_space, n_tm, *refs),
            out_shape=jax.ShapeDtypeStruct((2, 1, n_mom), f32),
            in_specs=[pl.BlockSpec(memory_space=pl.ANY)] * 4,
            out_specs=pl.BlockSpec(memory_space=pltpu.VMEM),
            scratch_shapes=scratch,
            compiler_params=pltpu.CompilerParams(
                collective_id=0, has_side_effects=True, vmem_limit_bytes=60 * 1024 * 1024
            ),
            name="loops",
        )(
            sources.reshape((2, 2, 4, 3) + tile),
            clover.reshape((2, 2, 6, 6) + tile),
            links.reshape((4, 2, 3, 3) + tile),
            momenta.T,
        )
        return out.reshape(2, 1, n_mom, 1)

    placed = P(None, None, None, None, "space", "tm", None)
    return jax.shard_map(
        local, mesh=mesh, in_specs=(placed, placed, placed, P()), out_specs=P(None, "space", None, "tm"), check_vma=False
    )
```

time: 66.1 us -> 57.5 us (0.87)
  Pallas kernels: 61.7 us -> 56.2 us
  local copies, waits for them, and re-layouts: 4.2 us -> 1.21 us
    pallas_call x1, Pallas kernels: 61.7 us -> 56.2 us  [local(): pl.pallas_call(lambda *refs: kernel(n_space, n_tm, *refs), out_shape=jax....]
    unnamed x9 -> x3, local copies, waits for them, and re-layouts: 4.2 us -> 1.21 us
where the time goes in v1:
time: 57.5 us; the launch traced here: 57.4 us
  Pallas kernels  56.2 us (98%)
  local copies, waits for them, and re-layouts  1.21 us (2%)
    pallas_call x1, Pallas kernels, local(): pl.pallas_call(lambda *refs: kernel(n_space, n_tm, *refs), out_shape=jax....  56.2 us
    unnamed x3, local copies, waits for them, and re-layouts  1.21 us

profile of v1, /device:TPU:1, one launch (start us, length us, event | category | flops | bytes accessed | tf_op | source)
XLA Modules:
  0.0 57.4 jit_solution(6842066380407261465)
XLA Ops:
  0.0 56.2 %loops.1 = f32[2,1,33]{2,1,0:T(1,128)} custom-call(f32[2,2,4,3,8,128]{5,4,3,2,1,0:T(8,128)} %bitcast.9, f32[2,2,6,6,8,128]{5,4,3,2,1,0:T(8,128)} %bitcast.7, f32[4,2,3,3,8,128]{5,4,3,2,1,0:T(8,128)} %bitcast.8, s32[3,33]{1,0:T(4,128)} %bitcast.11), custom_call_target="tpu_custom_call" | custom-call | tf_op jit(solution)/shard_map/loops/pallas_call | solution.py:572
  56.2 0.0 copy-start
  56.2 0.7 %copy-done = f32[2,1,33]{2,1,0:T(1,128)S(1)} copy-done((f32[2,1,33]{2,1,0:T(1,128)S(1)}, f32[2,1,33]{2,1,0:T(1,128)}, u32[]{:S(2)}) %copy-start) | copy-done | bytes 288
  56.8 0.6 copy.7
Async XLA Ops:
  56.2 0.7 %copy-start = (f32[2,1,33]{2,1,0:T(1,128)S(1)}, f32[2,1,33]{2,1,0:T(1,128)}, u32[]{:S(2)}) copy-start(f32[2,1,33]{2,1,0:T(1,128)} %loops.1) | copy-start | bytes 796

commit v2 on v1

--- a/solution.py
+++ b/solution.py
@@ -100,6 +100,7 @@
 ALONG_Y = fan(range(4), [0], [0], [0])
 ALONG_Z = fan([0], [0], [0], range(4))
 ALONG_SPACE = fan(range(4), range(4), range(2), [0])
+EVERYONE = fan(range(4), range(4), range(2), range(4))
 ROUNDS = (ALONG_ROW, ALONG_Y, ALONG_Z)
 
 
@@ -119,7 +120,7 @@
     n_space, n_tm,
     src_hbm, clov_hbm, link_hbm, mom_hbm, out_ref,
     src, clov, link, mom_ref, wlink, wclov, sfield, field, inner, base, bil, cur, phase_hi, phase_lo, momrow,
-    send, recv, row_s, row_r0, row_r1, row_r2, last_r1, last_r2, alpha_ref, loop_s, loop_r,
+    send, recv, row_s, row_r0, row_r1, row_r2, last_r, alpha_ref, loop_s, loop_r,
     in_sem, send_sem, recv_sem, row_ssem, row_rsem, loop_ssem, loop_rsem,
 ):
     x = lax.axis_index("space")
@@ -129,7 +130,7 @@
 
     loads = [
         pltpu.make_async_copy(a, b, in_sem.at[k])
-        for k, (a, b) in enumerate(((src_hbm, src), (clov_hbm, clov), (link_hbm, link), (mom_hbm, mom_ref)))
+        for k, (a, b) in enumerate(((src_hbm, src), (link_hbm, link), (clov_hbm, clov), (mom_hbm, mom_ref)))
     ]
     for load in loads:
         load.start()
@@ -142,9 +143,9 @@
         return (space_at(dy, dx, dc), (t + dz) & 3)
 
     barrier = pltpu.get_barrier_semaphore()
-    greeted = ALONG_SPACE + ALONG_Z
-    for offset in greeted:
-        pl.semaphore_signal(barrier, inc=1, device_id=place(offset), device_id_type=MESH)
+    greeted = [(x_up, t), (x_dn, t)] + [place(offset) for group in ROUNDS for offset in group]
+    for device in greeted:
+        pl.semaphore_signal(barrier, inc=1, device_id=device, device_id_type=MESH)
 
     lane = lax.broadcasted_iota(jnp.int32, (8, 128), 1)
     row = lax.broadcasted_iota(jnp.int32, (8, 128), 0)
@@ -477,12 +478,12 @@
         sfield[0, re_im] = jnp.where(ev, a, b)
         sfield[1, re_im] = jnp.where(ev, b, a)
     loads[1].wait()
+    pack_links((0, 3))
+    loads[2].wait()
     pack_clover(((1, 1),))
     cr, ci = clover_apply(wclov.at[1, 1], sfield[1, 0], sfield[1, 1])
     inner[4, 0] = cr
     inner[4, 1] = ci
-    loads[2].wait()
-    pack_links((0, 3))
     pl.semaphore_wait(barrier, len(greeted))
     hr, hi = hop(
         0, 1, cr, ci, lambda: pack_links((1, 2)), lambda: pack_clover(((0, 1), (0, 0), (1, 0)))
@@ -503,13 +504,11 @@
         a, b = jnp.sum(v * v, axis=(0, 1)), jnp.sum(v * w, axis=(0, 1))
         m1, m2 = (a, b) if m1 is None else (m1 + a, m2 + b)
     row_s[4, 0:1, :] = to_row([alpha_ref[1], m1, m2])
-    row_send(ALONG_Z, 4, last_r1, 3)
+    row_send(EVERYONE, 4, last_r, 3)
     second = x >= n_space // 2
     angle = momrow[0:1, :].astype(jnp.int32) * second.astype(jnp.int32)
     cos, sin = cos_sin(angle & 31)
     sin = jnp.where(lane1 < 64, -sin, sin)
-    row_s[5, 0:1, :] = row_recv(4, last_r1, 3)
-    row_send(ALONG_SPACE, 5, last_r2, 4)
     pltpu.make_async_copy(loop_r, loop_r, loop_rsem).wait()
     own = loop_s[pl.ds(pl.multiple_of(x * 8, 8), 8), :]
     piece = own + jnp.sum(loop_r[...], axis=0)
@@ -517,7 +516,7 @@
     piece = piece * (1.0 / math.sqrt(n_space * NY * NZ))
     start = row_s[3, 0:1, :]
     rr0, im0 = [jnp.where(second, v[1], v[0]) for v in (from_row(start, 0), from_row(start, 1))]
-    line = row_recv(5, last_r2, 4)
+    line = row_recv(4, last_r, 3)
     rr1, m1, m2 = [jnp.where(second, v[1], v[0]) for v in (from_row(line, 0), from_row(line, 1), from_row(line, 2))]
     alpha0, beta = rr0 / im0, rr1 / rr0
     alpha1 = rr1 / (m1 + beta * (2.0 * m2 + beta * im0))
@@ -526,7 +525,7 @@
     out_ref[1] = line[:, 64 : 64 + n_mom]
 
     pltpu.make_async_copy(send, send, send_sem).wait()
-    for stage, ref in enumerate((row_r0, row_r1, row_r2, last_r1, last_r2)):
+    for stage, ref in enumerate((row_r0, row_r1, row_r2, last_r)):
         pltpu.make_async_copy(ref, ref, row_ssem.at[stage]).wait()
     pltpu.make_async_copy(loop_r, loop_r, loop_ssem).wait()
 
@@ -557,7 +556,7 @@
             pltpu.VMEM((9, 4, 2, 2, 3) + tile, f32),
             pltpu.VMEM((9, 4, 2, 2, 3) + tile, f32),
             pltpu.VMEM((6,) + tile, f32),
-            *[pltpu.VMEM((len(group), 128), f32) for group in ROUNDS + (ALONG_Z, ALONG_SPACE)],
+            *[pltpu.VMEM((len(group), 128), f32) for group in ROUNDS + (EVERYONE,)],
             pltpu.VMEM((2,) + tile, f32),
             pltpu.VMEM((256, 128), f32),
             pltpu.VMEM((n_space - 1,) + tile, f32),
@@ -576,14 +575,19 @@
             out_specs=pl.BlockSpec(memory_space=pltpu.VMEM),
             scratch_shapes=scratch,
             compiler_params=pltpu.CompilerParams(
-                collective_id=0, has_side_effects=True, vmem_limit_bytes=60 * 1024 * 1024
+                collective_id=0, has_side_effects=True, vmem_limit_bytes=48 * 1024 * 1024
             ),
             name="loops",
         )(
-            sources.reshape((2, 2, 4, 3) + tile),
-            clover.reshape((2, 2, 6, 6) + tile),
-            links.reshape((4, 2, 3, 3) + tile),
-            momenta.T,
+            *[
+                pltpu.with_memory_space_constraint(v, pltpu.HBM)
+                for v in (
+                    sources.reshape((2, 2, 4, 3) + tile),
+                    clover.reshape((2, 2, 6, 6) + tile),
+                    links.reshape((4, 2, 3, 3) + tile),
+                    momenta.T,
+                )
+            ]
         )
         return out.reshape(2, 1, n_mom, 1)
 

time: 57.5 us -> 54.5 us (0.948)
  Pallas kernels: 56.2 us -> 53.8 us
  local copies, waits for them, and re-layouts: 1.21 us -> 0.56 us
    pallas_call x1, Pallas kernels: 56.2 us -> 53.8 us  [local(): pl.pallas_call(lambda *refs: kernel(n_space, n_tm, *refs), out_shape=jax....]
    unnamed x3 -> x1, local copies, waits for them, and re-layouts: 1.21 us -> 0.56 us
where the time goes in v2:
time: 54.5 us; the launch traced here: 54.4 us
  Pallas kernels  53.8 us (99%)
  local copies, waits for them, and re-layouts  0.56 us (1%)
    pallas_call x1, Pallas kernels, local(): pl.pallas_call(lambda *refs: kernel(n_space, n_tm, *refs), out_shape=jax....  53.8 us

profile of v2, /device:TPU:1, one launch (start us, length us, event | category | flops | bytes accessed | tf_op | source)
XLA Modules:
  0.0 54.4 jit_solution(8021107334360475664)
XLA Ops:
  0.0 53.8 %loops.1 = f32[2,1,33]{2,1,0:T(1,128)S(1)} custom-call(f32[2,2,4,3,8,128]{5,4,3,2,1,0:T(8,128)} %bitcast.10, f32[2,2,6,6,8,128]{5,4,3,2,1,0:T(8,128)} %bitcast.8, f32[4,2,3,3,8,128]{5,4,3,2,1,0:T(8,128)} %bitcast.9, s32[3,33]{1,0:T(4,128)} %bitcast.11), custom_call_target="tpu_custom_call" | custom-call | tf_op jit(solution)/shard_map/loops/pallas_call | solution.py:571
  53.8 0.6 %copy.7 = f32[2,1,33,1]{2,3,1,0:T(1,128)} copy(f32[2,1,33,1]{2,3,1,0:T(1,128)S(1)} %bitcast.7) | data formatting | bytes 528

commit v3 on v2

--- a/solution.py
+++ b/solution.py
@@ -13,7 +13,6 @@
 NY = 32
 KAPPA = 0.1
 MOM = 48
-UNROLL = True
 
 
 UPPER = (((1, 1), (0, 1)), ((1, 0), (0, 2)), ((0, 1), (1, 3)), ((0, 0), (1, 0)))
@@ -80,15 +79,23 @@
     return outr, outi
 
 
-def clover_apply(mat, fr, fi):
+def clover_apply(mat, fr, fi, adjoint):
     xr, xi = fr.reshape(2, 6, 8, 128), fi.reshape(2, 6, 8, 128)
     outr = outi = None
     for i in range(6):
-        cr, ci = mat[0, :, :, i], mat[1, :, :, i]
         vr, vi = xr[:, i][:, None], xi[:, i][:, None]
-        tr, ti = cr * vr - ci * vi, cr * vi + ci * vr
+        if adjoint:
+            cr, ci = mat[0, :, i], mat[1, :, i]
+            tr, ti = cr * vr + ci * vi, cr * vi - ci * vr
+        else:
+            cr, ci = mat[0, :, :, i], mat[1, :, :, i]
+            tr, ti = cr * vr - ci * vi, cr * vi + ci * vr
         outr, outi = (tr, ti) if outr is None else (outr + tr, outi + ti)
     return outr.reshape(4, 3, 8, 128), outi.reshape(4, 3, 8, 128)
+
+
+def flip(v):
+    return jnp.concatenate([v[:2], -v[2:]], axis=0)
 
 
 def fan(ys, xs, cores, zs):
@@ -104,24 +111,12 @@
 ROUNDS = (ALONG_ROW, ALONG_Y, ALONG_Z)
 
 
-def when(condition):
-    if isinstance(condition, bool):
-        return (lambda f: f()) if condition else (lambda f: None)
-    return pl.when(condition)
-
-
-def pick(condition, a, b):
-    if isinstance(condition, bool):
-        return a if condition else b
-    return jnp.where(condition, a, b)
-
-
 def kernel(
     n_space, n_tm,
     src_hbm, clov_hbm, link_hbm, mom_hbm, out_ref,
     src, clov, link, mom_ref, wlink, wclov, sfield, field, inner, base, bil, cur, phase_hi, phase_lo, momrow,
-    send, recv, row_s, row_r0, row_r1, row_r2, last_r, alpha_ref, loop_s, loop_r,
-    in_sem, send_sem, recv_sem, row_ssem, row_rsem, loop_ssem, loop_rsem,
+    send, recv, row_s, row_r0, row_r1, row_r2, last_r, alpha_ref, loop_s, loop_r, far_clov, far_link, far_send, far_recv, far_raw, echo,
+    in_sem, send_sem, recv_sem, row_ssem, row_rsem, loop_ssem, loop_rsem, far_ssem, far_rsem,
 ):
     x = lax.axis_index("space")
     t = lax.axis_index("tm")
@@ -178,18 +173,12 @@
             c = 1.0 / math.factorial(m) - q * c
         return 2.0 * s * s - 1.0, -2.0 * s * c
 
-    def pack_clover(entries):
+    def pack_clover(par):
         def step(k, carry):
             re_im, chi, r = k // 12, (k // 6) % 2, k % 6
-            sign = (1 - 2 * re_im).astype(jnp.float32)
             a = clov[re_im, chi, r]
             b = move(a, 2, -1)
-            for forward, par in entries:
-                v = jnp.where(ev, a, b) if par == 0 else jnp.where(ev, b, a)
-                if forward:
-                    wclov[1, par, re_im, chi, r] = v
-                else:
-                    wclov[0, par, re_im, chi, :, r] = v * sign
+            wclov[par, re_im, chi, r] = jnp.where(ev, a, b) if par == 0 else jnp.where(ev, b, a)
             return carry
 
         lax.fori_loop(0, 24, step, 0)
@@ -243,14 +232,6 @@
         field[5, 0] = zero
         field[5, 1] = zero
 
-    ROUTES = ((0, -1, (x_dn, t)), (0, 1, (x_up, t)), (3, -1, (x, t_dn)), (3, 1, (x, t_up)))
-
-    def halo(j, k):
-        return pltpu.make_async_remote_copy(
-            src_ref=send.at[j, k], dst_ref=recv.at[j, k], send_sem=send_sem, recv_sem=recv_sem.at[j, k],
-            device_id=ROUTES[k][2], device_id_type=MESH,
-        )
-
     def project(fr, fi, mu, sign):
         rows_r, rows_i = [], []
         for spin in range(2):
@@ -271,33 +252,6 @@
                 power += 2
             term = (hr[col], hi[col])
             acc[2 + spin] = times_i(power, *term) if acc[2 + spin] is None else add_times_i(power, acc[2 + spin], term)
-
-    def hop(j, par, fr, fi, early, late):
-        to = 1 - par
-        for k, (mu, sign, _) in enumerate(ROUTES):
-            half = project(fr, fi, mu, sign)
-            if sign > 0:
-                half = color_apply(wlink.at[par, mu], half, True)
-            send[j, k, 0] = half[0]
-            send[j, k, 1] = half[1]
-            halo(j, k).start()
-        early()
-        acc = [None] * 4
-        for mu in (1, 2):
-            hr, hi = project(fr, fi, mu, -1)
-            ahead = (move(hr, mu, 1), move(hi, mu, 1))
-            add_up(acc, color_apply(wlink.at[to, mu], ahead, False), mu, -1)
-            hr, hi = color_apply(wlink.at[par, mu], project(fr, fi, mu, 1), True)
-            add_up(acc, (move(hr, mu, -1), move(hi, mu, -1)), mu, 1)
-        late()
-        for k in (2, 3, 0, 1):
-            mu, sign, _ = ROUTES[k]
-            halo(j, k).wait_recv()
-            half = (recv[j, k, 0], recv[j, k, 1])
-            if sign < 0:
-                half = color_apply(wlink.at[to, mu], half, False)
-            add_up(acc, half, mu, sign)
-        return jnp.stack([a[0] for a in acc]), jnp.stack([a[1] for a in acc])
 
     def to_row(tiles):
         out = jnp.zeros((8, 128), jnp.float32)
@@ -385,43 +339,144 @@
                 send_sem=loop_ssem, recv_sem=loop_rsem, device_id=(target, t), device_id_type=MESH,
             ).start()
 
-    def nothing():
-        pass
-
-    def pair(p, carry):
-        forward = p % 2
-        g5 = 2.0 * forward - 1.0 if isinstance(p, int) else (2 * forward - 1).astype(jnp.float32)
-
-        def flip(v):
-            return jnp.concatenate([v[:2], v[2:] * g5], axis=0)
-
-        def early_a():
-            @when(p == 2)
-            def _():
+    def main(core):
+        far, near = (x_dn, x_up) if core == 0 else (x_up, x_dn)
+        devices = ((far, t), (near, t), (x, t_dn), (x, t_up))
+        sign_in = (1, -1, -1, 1) if core == 0 else (-1, 1, -1, 1)
+        sign_out = (-1, 1, -1, 1) if core == 0 else (1, -1, -1, 1)
+        axes = (0, 0, 3, 3)
+
+        def copy(j, k):
+            return pltpu.make_async_remote_copy(
+                src_ref=send.at[j, k], dst_ref=recv.at[j, k], send_sem=send_sem, recv_sem=recv_sem.at[j, k],
+                device_id=devices[k], device_id_type=MESH,
+            )
+
+        def post(j, k, par, fr, fi):
+            half = project(fr, fi, axes[k], sign_out[k])
+            if sign_out[k] > 0:
+                half = color_apply(wlink.at[par, axes[k]], half, True)
+            send[j, k, 0] = half[0]
+            send[j, k, 1] = half[1]
+            copy(j, k).start()
+
+        def take(acc, j, k, to):
+            copy(j, k).wait_recv()
+            half = (recv[j, k, 0], recv[j, k, 1])
+            if k == 0 and j > 0:
+                half = (half[0] + echo[0], half[1] + echo[1])
+            if sign_in[k] < 0:
+                half = color_apply(wlink.at[to, axes[k]], half, False)
+            add_up(acc, half, axes[k], sign_in[k])
+
+        def stacked(acc):
+            return jnp.stack([a[0] for a in acc]), jnp.stack([a[1] for a in acc])
+
+        def message(j):
+            if j == 0:
+                return inner[4, 0], inner[4, 1]
+            p = (j - 1) // 2
+            if j % 2 == 0:
+                return inner[p, 0], inner[p, 1]
+            if p % 2 == 0:
+                return flip(field[p, 0]), flip(field[p, 1])
+            return field[p, 0], field[p, 1]
+
+        def linear(j, fr, fi, clover):
+            if j == 0:
+                return KAPPA * fr, KAPPA * fi
+            adjoint = (j - 1) // 2 % 2 == 0
+            if j % 2 == 1:
+                fr, fi = clover_apply(clover, fr, fi, adjoint)
+                return KAPPA * fr, KAPPA * fi
+            if adjoint:
+                fr, fi = flip(fr), flip(fi)
+            return -KAPPA * fr, -KAPPA * fi
+
+        def outgoing(j, fr, fi):
+            if j % 4 == 0:
+                return flip(fr), flip(fi)
+            return fr, fi
+
+        def far_copy(k):
+            src, dst = (far_send.at[k], far_recv.at[k]) if k < 2 else (link.at[0], far_raw)
+            return pltpu.make_async_remote_copy(
+                src_ref=src, dst_ref=dst, send_sem=far_ssem.at[k], recv_sem=far_rsem.at[k],
+                device_id=devices[0], device_id_type=MESH,
+            )
+
+        def make_echo(j):
+            par = j % 2
+            if j == 1 and core == 0:
+                far_copy(2).wait_recv()
+                a = far_raw[...]
+                b = move(a, 2, -1)
+                far_link[0] = jnp.where(ev, b, a)
+                far_link[1] = jnp.where(ev, a, b)
+            if j == 2:
+                for chi in range(2):
+                    far_copy(chi).wait_recv()
+
+                    def unpack(r, carry):
+                        a = far_recv[chi, r]
+                        far_clov[0, chi, r] = jnp.where(ev, a, move(a, 2, -1))
+                        far_clov[1, chi, r] = jnp.where(ev, move(a, 2, 1), a)
+                        return carry
+
+                    lax.fori_loop(0, 6, unpack, 0)
+            half = project(*message(j - 1), 0, sign_out[0])
+            if core == 1:
+                half = color_apply(wlink.at[par, 0], half, True)
+            else:
+                half = color_apply(far_link.at[1 - par], half, False)
+            acc = [None] * 4
+            add_up(acc, half, 0, sign_out[0])
+            fr, fi = outgoing(j - 1, *linear(j - 1, *stacked(acc), far_clov))
+            half = project(fr, fi, 0, sign_in[0])
+            if core == 0:
+                half = color_apply(far_link.at[1 - par], half, True)
+            echo[0] = half[0]
+            echo[1] = half[1]
+
+        def early(j):
+            if j == 0:
+                if core == 1:
+                    far_copy(2).start()
+                for chi in range(2):
+
+                    def pack(r, carry):
+                        far_send[chi, r] = jnp.where(ev, wclov[1, 1, chi, r], wclov[1, 0, chi, r])
+                        return carry
+
+                    lax.fori_loop(0, 6, pack, 0)
+                far_copy(0).start()
+                pack_links((1, 2))
+            if j == 1:
+                far_copy(1).start()
+            if j == 5:
+                r0, r1 = field[1, 0], field[1, 1]
+                i0, i1 = field[2, 0], field[2, 1]
+                row_s[0, 0:1, :] = to_row([jnp.sum(a * a + b * b, axis=(0, 1)) for a, b in ((r0, r1), (i0, i1))])
                 row_send(ROUNDS[0], 0, first_r[0], 0)
-
-            @when(p == 3)
-            def _():
-                row_send(ROUNDS[2], 2, first_r[2], 2)
-
-        def late_a():
-            @when(p == 0)
-            def _():
+            if j in (6, 7):
+                row_s[j - 5, 0:1, :] = row_recv(j - 6, first_r[j - 6], j - 6)
+                row_send(ROUNDS[j - 5], j - 5, first_r[j - 5], j - 5)
+
+        def late(j):
+            if j == 0:
+                pack_clover(0)
+            if j == 1:
                 make_phases()
-
-        def early_b():
-            @when(p == 2)
-            def _():
-                row_s[1, 0:1, :] = row_recv(0, first_r[0], 0)
-                row_send(ROUNDS[1], 1, first_r[1], 1)
-
-        def late_b():
-            cr, ci = clover_apply(wclov.at[forward, 0], field[p, 0], field[p, 1])
-            base[0] = cr
-            base[1] = ci
-
-            @when(p == 3)
-            def _():
+            if j > 0 and j % 2 == 0:
+                p = j // 2 - 1
+                cr, ci = clover_apply(wclov.at[0], field[p, 0], field[p, 1], p % 2 == 0)
+                base[0] = cr
+                base[1] = ci
+            if j == 4:
+                project_loops(0, 5, 4)
+            if j == 6:
+                project_loops(1, 1, 1)
+            if j == 8:
                 line = row_recv(2, first_r[2], 2)
                 row_s[3, 0:1, :] = line
                 rr, image = from_row(line, 0), from_row(line, 1)
@@ -433,43 +488,46 @@
                     r = field[1, re_im] - alpha * field[3, re_im]
                     field[6, re_im] = r
                     inner[5, re_im] = inner[1, re_im] - alpha_odd * inner[3, re_im]
-                    s = jnp.sum(r * r, axis=(0, 1))
-                    sq = s if sq is None else sq + s
+                    part = jnp.sum(r * r, axis=(0, 1))
+                    sq = part if sq is None else sq + part
                 alpha_ref[1] = sq
-
-            @when(p > 0)
-            def _():
-                at_field = pick(p == 1, 5, pick(p == 2, 1, 6))
-                at_inner = pick(p == 1, 4, pick(p == 2, 1, 5))
-                project_loops(p - 1, at_field, at_inner)
-
-            @when(p == 3)
-            def _():
+                project_loops(2, 6, 5)
                 loops_send()
 
-        fr, fi = field[p, 0], field[p, 1]
-        hr, hi = hop(2 * p + 1, 0, flip(fr), flip(fi), early_a, late_a)
-        vr, vi = clover_apply(wclov.at[forward, 1], hr, hi)
-        vr, vi = KAPPA * vr, KAPPA * vi
-        inner[p, 0] = vr
-        inner[p, 1] = vi
-        hr, hi = hop(2 * p + 2, 1, vr, vi, early_b, late_b)
-        outr, outi = base[0] - KAPPA * flip(hr), base[1] - KAPPA * flip(hi)
-        field[p + 1, 0] = outr
-        field[p + 1, 1] = outi
-
-        @when(p == 1)
-        def _():
-            r0, r1 = field[1, 0], field[1, 1]
-            i0, i1 = field[2, 0], field[2, 1]
-            tiles = [jnp.sum(a * a + b * b, axis=(0, 1)) for a, b in ((r0, r1), (i0, i1))]
-            row_s[0, 0:1, :] = to_row(tiles)
-
-        @when(p == 2)
-        def _():
-            row_s[2, 0:1, :] = row_recv(1, first_r[1], 1)
-
-        return carry
+        post(0, 0, 1, *message(0))
+        for j in range(9):
+            par, to = 1 - j % 2, j % 2
+            p = (j - 1) // 2
+            fr, fi = message(j)
+            for k in (2, 3, 1):
+                post(j, k, par, fr, fi)
+            early(j)
+            acc = [None] * 4
+            for mu in (1, 2):
+                hr, hi = project(fr, fi, mu, -1)
+                ahead = (move(hr, mu, 1), move(hi, mu, 1))
+                add_up(acc, color_apply(wlink.at[to, mu], ahead, False), mu, -1)
+                hr, hi = color_apply(wlink.at[par, mu], project(fr, fi, mu, 1), True)
+                add_up(acc, (move(hr, mu, -1), move(hi, mu, -1)), mu, 1)
+            if j > 0:
+                make_echo(j)
+            late(j)
+            for k in (1, 2, 3):
+                take(acc, j, k, to)
+            vr, vi = linear(j, *stacked(acc), wclov.at[1])
+            if j % 2 == 0:
+                start = (base[0], base[1]) if j > 0 else (sfield[0, 0], sfield[0, 1])
+                vr, vi = start[0] + vr, start[1] + vi
+            if j < 8:
+                post(j + 1, 0, to, *outgoing(j, vr, vi))
+            acc = [None] * 4
+            take(acc, j, 0, to)
+            lr, li = linear(j, *stacked(acc), wclov.at[1])
+            store, at = (field, j // 2) if j % 2 == 0 else (inner, p)
+            store[at, 0] = vr + lr
+            store[at, 1] = vi + li
+        for k in range(2 + core):
+            far_copy(k).wait_send()
 
     loads[0].wait()
     for re_im in range(2):
@@ -480,22 +538,13 @@
     loads[1].wait()
     pack_links((0, 3))
     loads[2].wait()
-    pack_clover(((1, 1),))
-    cr, ci = clover_apply(wclov.at[1, 1], sfield[1, 0], sfield[1, 1])
+    pack_clover(1)
+    cr, ci = clover_apply(wclov.at[1], sfield[1, 0], sfield[1, 1], False)
     inner[4, 0] = cr
     inner[4, 1] = ci
     pl.semaphore_wait(barrier, len(greeted))
-    hr, hi = hop(
-        0, 1, cr, ci, lambda: pack_links((1, 2)), lambda: pack_clover(((0, 1), (0, 0), (1, 0)))
-    )
-    field[0, 0] = sfield[0, 0] + KAPPA * hr
-    field[0, 1] = sfield[0, 1] + KAPPA * hi
-
-    if UNROLL:
-        for p in range(4):
-            pair(p, 0)
-    else:
-        lax.fori_loop(0, 4, pair, 0)
+    for core in range(2):
+        pl.when(x % 2 == core)(lambda core=core: main(core))
 
     alpha = alpha_ref[0]
     m1 = m2 = None
@@ -543,7 +592,7 @@
             pltpu.VMEM((4, 2, 3, 3) + tile, f32),
             pltpu.VMEM((3, n_mom), jnp.int32),
             pltpu.VMEM((2, 4, 2, 3, 3) + tile, f32),
-            pltpu.VMEM((2, 2, 2, 2, 6, 6) + tile, f32),
+            pltpu.VMEM((2, 2, 2, 6, 6) + tile, f32),
             pltpu.VMEM((2, 2, 4, 3) + tile, f32),
             pltpu.VMEM((7, 2, 4, 3) + tile, f32),
             pltpu.VMEM((6, 2, 4, 3) + tile, f32),
@@ -560,6 +609,12 @@
             pltpu.VMEM((2,) + tile, f32),
             pltpu.VMEM((256, 128), f32),
             pltpu.VMEM((n_space - 1,) + tile, f32),
+            pltpu.VMEM((2, 2, 6, 6) + tile, f32),
+            pltpu.VMEM((2, 2, 3, 3) + tile, f32),
+            pltpu.VMEM((2, 6, 6) + tile, f32),
+            pltpu.VMEM((2, 6, 6) + tile, f32),
+            pltpu.VMEM((2, 3, 3) + tile, f32),
+            pltpu.VMEM((2, 2, 3) + tile, f32),
             pltpu.SemaphoreType.DMA((4,)),
             pltpu.SemaphoreType.DMA,
             pltpu.SemaphoreType.DMA((9, 4)),
@@ -567,6 +622,8 @@
             pltpu.SemaphoreType.DMA((5,)),
             pltpu.SemaphoreType.DMA,
             pltpu.SemaphoreType.DMA,
+            pltpu.SemaphoreType.DMA((3,)),
+            pltpu.SemaphoreType.DMA((3,)),
         ]
         out = pl.pallas_call(
             lambda *refs: kernel(n_space, n_tm, *refs),

time: 54.5 us -> 52 us (0.954)
  Pallas kernels: 53.8 us -> 51.3 us
    pallas_call x1, Pallas kernels: 53.8 us -> 51.3 us  [local(): pl.pallas_call(lambda *refs: kernel(n_space, n_tm, *refs), out_shape=jax....]
where the time goes in v3:
time: 52 us; the launch traced here: 51.8 us
  Pallas kernels  51.3 us (99%)
  local copies, waits for them, and re-layouts  0.56 us (1%)
    pallas_call x1, Pallas kernels, local(): pl.pallas_call(lambda *refs: kernel(n_space, n_tm, *refs), out_shape=jax....  51.3 us

profile of v3, /device:TPU:1, one launch (start us, length us, event | category | flops | bytes accessed | tf_op | source)
XLA Modules:
  0.0 51.8 jit_solution(1091253287796215040)
XLA Ops:
  0.0 51.3 %loops.1 = f32[2,1,33]{2,1,0:T(1,128)S(1)} custom-call(f32[2,2,4,3,8,128]{5,4,3,2,1,0:T(8,128)} %bitcast.10, f32[2,2,6,6,8,128]{5,4,3,2,1,0:T(8,128)} %bitcast.8, f32[4,2,3,3,8,128]{5,4,3,2,1,0:T(8,128)} %bitcast.9, s32[3,33]{1,0:T(4,128)} %bitcast.11), custom_call_target="tpu_custom_call" | custom-call | tf_op jit(solution)/shard_map/loops/pallas_call | solution.py:628
  51.3 0.6 %copy.7 = f32[2,1,33,1]{2,3,1,0:T(1,128)} copy(f32[2,1,33,1]{2,3,1,0:T(1,128)S(1)} %bitcast.7) | data formatting | bytes 528

commit v4 on v3

--- a/solution.py
+++ b/solution.py
@@ -12,6 +12,8 @@
 NZ = 32
 NY = 32
 KAPPA = 0.1
+HALVES = (slice(0, 4), slice(4, 8))
+PARTS = (HALVES, (slice(0, 8),), HALVES, HALVES)
 MOM = 48
 
 
@@ -80,7 +82,8 @@
 
 
 def clover_apply(mat, fr, fi, adjoint):
-    xr, xi = fr.reshape(2, 6, 8, 128), fi.reshape(2, 6, 8, 128)
+    tile = fr.shape[2:]
+    xr, xi = fr.reshape((2, 6) + tile), fi.reshape((2, 6) + tile)
     outr = outi = None
     for i in range(6):
         vr, vi = xr[:, i][:, None], xi[:, i][:, None]
@@ -91,7 +94,7 @@
             cr, ci = mat[0, :, :, i], mat[1, :, :, i]
             tr, ti = cr * vr - ci * vi, cr * vi + ci * vr
         outr, outi = (tr, ti) if outr is None else (outr + tr, outi + ti)
-    return outr.reshape(4, 3, 8, 128), outi.reshape(4, 3, 8, 128)
+    return outr.reshape((4, 3) + tile), outi.reshape((4, 3) + tile)
 
 
 def flip(v):
@@ -115,7 +118,7 @@
     n_space, n_tm,
     src_hbm, clov_hbm, link_hbm, mom_hbm, out_ref,
     src, clov, link, mom_ref, wlink, wclov, sfield, field, inner, base, bil, cur, phase_hi, phase_lo, momrow,
-    send, recv, row_s, row_r0, row_r1, row_r2, last_r, alpha_ref, loop_s, loop_r, far_clov, far_link, far_send, far_recv, far_raw, echo,
+    send, recv, row_s, row_r0, row_r1, row_r2, last_r, alpha_ref, loop_s, loop_r, far_clov, far_link, far_send, far_recv, far_raw, echo, partial,
     in_sem, send_sem, recv_sem, row_ssem, row_rsem, loop_ssem, loop_rsem, far_ssem, far_rsem,
 ):
     x = lax.axis_index("space")
@@ -335,7 +338,7 @@
         for k, offset in enumerate(ALONG_SPACE):
             target, _ = place(offset)
             pltpu.make_async_remote_copy(
-                src_ref=loop_s.at[pl.ds(pl.multiple_of(target * 8, 8), 8)], dst_ref=loop_r.at[k],
+                src_ref=loop_s.at[pl.ds(pl.multiple_of(target * 8, 8), 3)], dst_ref=loop_r.at[k, pl.ds(0, 3)],
                 send_sem=loop_ssem, recv_sem=loop_rsem, device_id=(target, t), device_id_type=MESH,
             ).start()
 
@@ -346,41 +349,43 @@
         sign_out = (-1, 1, -1, 1) if core == 0 else (1, -1, -1, 1)
         axes = (0, 0, 3, 3)
 
-        def copy(j, k):
+        def copy(j, k, part):
+            at = PARTS[k][part]
             return pltpu.make_async_remote_copy(
-                src_ref=send.at[j, k], dst_ref=recv.at[j, k], send_sem=send_sem, recv_sem=recv_sem.at[j, k],
-                device_id=devices[k], device_id_type=MESH,
+                src_ref=send.at[j, k, :, :, :, at], dst_ref=recv.at[j, k, :, :, :, at], send_sem=send_sem,
+                recv_sem=recv_sem.at[j, k, part], device_id=devices[k], device_id_type=MESH,
             )
 
-        def post(j, k, par, fr, fi):
+        def post(j, k, part, par, fr, fi):
+            at = PARTS[k][part]
             half = project(fr, fi, axes[k], sign_out[k])
             if sign_out[k] > 0:
-                half = color_apply(wlink.at[par, axes[k]], half, True)
-            send[j, k, 0] = half[0]
-            send[j, k, 1] = half[1]
-            copy(j, k).start()
-
-        def take(acc, j, k, to):
-            copy(j, k).wait_recv()
-            half = (recv[j, k, 0], recv[j, k, 1])
+                half = color_apply(wlink.at[par, axes[k], :, :, :, at], half, True)
+            send[j, k, 0, :, :, at] = half[0]
+            send[j, k, 1, :, :, at] = half[1]
+            copy(j, k, part).start()
+
+        def take(acc, j, k, part, to):
+            at = PARTS[k][part]
+            copy(j, k, part).wait_recv()
+            half = (recv[j, k, 0, :, :, at], recv[j, k, 1, :, :, at])
             if k == 0 and j > 0:
-                half = (half[0] + echo[0], half[1] + echo[1])
+                half = (half[0] + echo[0, :, :, at], half[1] + echo[1, :, :, at])
             if sign_in[k] < 0:
-                half = color_apply(wlink.at[to, axes[k]], half, False)
+                half = color_apply(wlink.at[to, axes[k], :, :, :, at], half, False)
             add_up(acc, half, axes[k], sign_in[k])
 
         def stacked(acc):
             return jnp.stack([a[0] for a in acc]), jnp.stack([a[1] for a in acc])
 
-        def message(j):
+        def message(j, at=slice(0, 8)):
             if j == 0:
-                return inner[4, 0], inner[4, 1]
+                return inner[4, 0, :, :, at], inner[4, 1, :, :, at]
             p = (j - 1) // 2
             if j % 2 == 0:
-                return inner[p, 0], inner[p, 1]
-            if p % 2 == 0:
-                return flip(field[p, 0]), flip(field[p, 1])
-            return field[p, 0], field[p, 1]
+                return inner[p, 0, :, :, at], inner[p, 1, :, :, at]
+            fr, fi = field[p, 0, :, :, at], field[p, 1, :, :, at]
+            return (flip(fr), flip(fi)) if p % 2 == 0 else (fr, fi)
 
         def linear(j, fr, fi, clover):
             if j == 0:
@@ -442,6 +447,7 @@
             if j == 0:
                 if core == 1:
                     far_copy(2).start()
+                pack_clover(1)
                 for chi in range(2):
 
                     def pack(r, carry):
@@ -494,13 +500,16 @@
                 project_loops(2, 6, 5)
                 loops_send()
 
-        post(0, 0, 1, *message(0))
+        for part in range(2):
+            post(0, 0, part, 1, *message(0, HALVES[part]))
+        for part in range(2):
+            for k in (2, 3):
+                post(0, k, part, 1, *message(0, HALVES[part]))
         for j in range(9):
             par, to = 1 - j % 2, j % 2
             p = (j - 1) // 2
             fr, fi = message(j)
-            for k in (2, 3, 1):
-                post(j, k, par, fr, fi)
+            post(j, 1, 0, par, fr, fi)
             early(j)
             acc = [None] * 4
             for mu in (1, 2):
@@ -512,20 +521,32 @@
             if j > 0:
                 make_echo(j)
             late(j)
-            for k in (1, 2, 3):
-                take(acc, j, k, to)
-            vr, vi = linear(j, *stacked(acc), wclov.at[1])
-            if j % 2 == 0:
-                start = (base[0], base[1]) if j > 0 else (sfield[0, 0], sfield[0, 1])
-                vr, vi = start[0] + vr, start[1] + vi
-            if j < 8:
-                post(j + 1, 0, to, *outgoing(j, vr, vi))
-            acc = [None] * 4
-            take(acc, j, 0, to)
-            lr, li = linear(j, *stacked(acc), wclov.at[1])
-            store, at = (field, j // 2) if j % 2 == 0 else (inner, p)
-            store[at, 0] = vr + lr
-            store[at, 1] = vi + li
+            take(acc, j, 1, 0, to)
+            partial[0], partial[1] = stacked(acc)
+            for part, at in enumerate(HALVES):
+                acc = [(partial[0, spin, :, at], partial[1, spin, :, at]) for spin in range(4)]
+                for k in (2, 3):
+                    take(acc, j, k, part, to)
+                vr, vi = linear(j, *stacked(acc), wclov.at[1, :, :, :, :, at])
+                if j % 2 == 0:
+                    start, first = (base, ()) if j > 0 else (sfield, (0,))
+                    vr = start[first + (0, slice(None), slice(None), at)] + vr
+                    vi = start[first + (1, slice(None), slice(None), at)] + vi
+                partial[0, :, :, at] = vr
+                partial[1, :, :, at] = vi
+                if j < 8:
+                    post(j + 1, 0, part, to, *outgoing(j, vr, vi))
+            for part, at in enumerate(HALVES):
+                acc = [None] * 4
+                take(acc, j, 0, part, to)
+                lr, li = linear(j, *stacked(acc), wclov.at[1, :, :, :, :, at])
+                vr, vi = partial[0, :, :, at] + lr, partial[1, :, :, at] + li
+                store, slot = (field, j // 2) if j % 2 == 0 else (inner, p)
+                store[slot, 0, :, :, at] = vr
+                store[slot, 1, :, :, at] = vi
+                if j < 8:
+                    for k in (2, 3):
+                        post(j + 1, k, part, to, *outgoing(j, vr, vi))
         for k in range(2 + core):
             far_copy(k).wait_send()
 
@@ -538,10 +559,9 @@
     loads[1].wait()
     pack_links((0, 3))
     loads[2].wait()
-    pack_clover(1)
-    cr, ci = clover_apply(wclov.at[1], sfield[1, 0], sfield[1, 1], False)
-    inner[4, 0] = cr
-    inner[4, 1] = ci
+    both = [clover_apply(clov, src[n, 0], src[n, 1], False) for n in range(2)]
+    for re_im in range(2):
+        inner[4, re_im] = jnp.where(ev, move(both[1][re_im], 2, -1), both[0][re_im])
     pl.semaphore_wait(barrier, len(greeted))
     for core in range(2):
         pl.when(x % 2 == core)(lambda core=core: main(core))
@@ -558,9 +578,10 @@
     angle = momrow[0:1, :].astype(jnp.int32) * second.astype(jnp.int32)
     cos, sin = cos_sin(angle & 31)
     sin = jnp.where(lane1 < 64, -sin, sin)
-    pltpu.make_async_copy(loop_r, loop_r, loop_rsem).wait()
-    own = loop_s[pl.ds(pl.multiple_of(x * 8, 8), 8), :]
-    piece = own + jnp.sum(loop_r[...], axis=0)
+    pieces = loop_r.at[:, pl.ds(0, 3)]
+    pltpu.make_async_copy(pieces, pieces, loop_rsem).wait()
+    own = loop_s[pl.ds(pl.multiple_of(x * 8, 8), 3), :]
+    piece = own + jnp.sum(loop_r[:, 0:3, :], axis=0)
     piece = piece * cos + pltpu.roll(piece, 64, 1) * sin
     piece = piece * (1.0 / math.sqrt(n_space * NY * NZ))
     start = row_s[3, 0:1, :]
@@ -576,7 +597,7 @@
     pltpu.make_async_copy(send, send, send_sem).wait()
     for stage, ref in enumerate((row_r0, row_r1, row_r2, last_r)):
         pltpu.make_async_copy(ref, ref, row_ssem.at[stage]).wait()
-    pltpu.make_async_copy(loop_r, loop_r, loop_ssem).wait()
+    pltpu.make_async_copy(pieces, pieces, loop_ssem).wait()
 
 
 def solution(mesh):
@@ -615,9 +636,10 @@
             pltpu.VMEM((2, 6, 6) + tile, f32),
             pltpu.VMEM((2, 3, 3) + tile, f32),
             pltpu.VMEM((2, 2, 3) + tile, f32),
+            pltpu.VMEM((2, 4, 3) + tile, f32),
             pltpu.SemaphoreType.DMA((4,)),
             pltpu.SemaphoreType.DMA,
-            pltpu.SemaphoreType.DMA((9, 4)),
+            pltpu.SemaphoreType.DMA((9, 4, 2)),
             pltpu.SemaphoreType.DMA((5,)),
             pltpu.SemaphoreType.DMA((5,)),
             pltpu.SemaphoreType.DMA,

time: 52 us -> 50.3 us (0.967)
  Pallas kernels: 51.3 us -> 49.6 us
    pallas_call x1, Pallas kernels: 51.3 us -> 49.6 us  [local(): pl.pallas_call(lambda *refs: kernel(n_space, n_tm, *refs), out_shape=jax....]
where the time goes in v4:
time: 50.3 us; the launch traced here: 50.2 us
  Pallas kernels  49.6 us (99%)
  local copies, waits for them, and re-layouts  0.56 us (1%)
    pallas_call x1, Pallas kernels, local(): pl.pallas_call(lambda *refs: kernel(n_space, n_tm, *refs), out_shape=jax....  49.6 us

profile of v4, /device:TPU:1, one launch (start us, length us, event | category | flops | bytes accessed | tf_op | source)
XLA Modules:
  0.0 50.2 jit_solution(8695267679313743770)
XLA Ops:
  0.0 49.6 %loops.1 = f32[2,1,33]{2,1,0:T(1,128)S(1)} custom-call(f32[2,2,4,3,8,128]{5,4,3,2,1,0:T(8,128)} %bitcast.10, f32[2,2,6,6,8,128]{5,4,3,2,1,0:T(8,128)} %bitcast.8, f32[4,2,3,3,8,128]{5,4,3,2,1,0:T(8,128)} %bitcast.9, s32[3,33]{1,0:T(4,128)} %bitcast.11), custom_call_target="tpu_custom_call" | custom-call | tf_op jit(solution)/shard_map/loops/pallas_call | solution.py:650
  49.6 0.6 %copy.7 = f32[2,1,33,1]{2,3,1,0:T(1,128)} copy(f32[2,1,33,1]{2,3,1,0:T(1,128)S(1)} %bitcast.7) | data formatting | bytes 528

commit v5 on v4

--- a/solution.py
+++ b/solution.py
@@ -541,10 +541,19 @@
                 take(acc, j, 0, part, to)
                 lr, li = linear(j, *stacked(acc), wclov.at[1, :, :, :, :, at])
                 vr, vi = partial[0, :, :, at] + lr, partial[1, :, :, at] + li
-                store, slot = (field, j // 2) if j % 2 == 0 else (inner, p)
-                store[slot, 0, :, :, at] = vr
-                store[slot, 1, :, :, at] = vi
-                if j < 8:
+                if j == 8:
+                    m1 = m2 = None
+                    for re_im, v in ((0, vr), (1, vi)):
+                        w = field[2, re_im, :, :, at]
+                        v = w - alpha_ref[0, at] * v
+                        a, b = jnp.sum(v * v, axis=(0, 1)), jnp.sum(v * w, axis=(0, 1))
+                        m1, m2 = (a, b) if m1 is None else (m1 + a, m2 + b)
+                    alpha_ref[2, at] = m1
+                    alpha_ref[3, at] = m2
+                else:
+                    store, slot = (field, j // 2) if j % 2 == 0 else (inner, p)
+                    store[slot, 0, :, :, at] = vr
+                    store[slot, 1, :, :, at] = vi
                     for k in (2, 3):
                         post(j + 1, k, part, to, *outgoing(j, vr, vi))
         for k in range(2 + core):
@@ -566,13 +575,7 @@
     for core in range(2):
         pl.when(x % 2 == core)(lambda core=core: main(core))
 
-    alpha = alpha_ref[0]
-    m1 = m2 = None
-    for re_im in range(2):
-        v, w = field[2, re_im] - alpha * field[4, re_im], field[2, re_im]
-        a, b = jnp.sum(v * v, axis=(0, 1)), jnp.sum(v * w, axis=(0, 1))
-        m1, m2 = (a, b) if m1 is None else (m1 + a, m2 + b)
-    row_s[4, 0:1, :] = to_row([alpha_ref[1], m1, m2])
+    row_s[4, 0:1, :] = to_row([alpha_ref[1], alpha_ref[2], alpha_ref[3]])
     row_send(EVERYONE, 4, last_r, 3)
     second = x >= n_space // 2
     angle = momrow[0:1, :].astype(jnp.int32) * second.astype(jnp.int32)
@@ -627,7 +630,7 @@
             pltpu.VMEM((9, 4, 2, 2, 3) + tile, f32),
             pltpu.VMEM((6,) + tile, f32),
             *[pltpu.VMEM((len(group), 128), f32) for group in ROUNDS + (EVERYONE,)],
-            pltpu.VMEM((2,) + tile, f32),
+            pltpu.VMEM((4,) + tile, f32),
             pltpu.VMEM((256, 128), f32),
             pltpu.VMEM((n_space - 1,) + tile, f32),
             pltpu.VMEM((2, 2, 6, 6) + tile, f32),

time: 50.3 us -> 50.4 us (level)
  no operation moved by 1% of the time
where the time goes in v5:
time: 50.4 us; the launch traced here: 50.2 us
  Pallas kernels  49.7 us (99%)
  local copies, waits for them, and re-layouts  0.56 us (1%)
    pallas_call x1, Pallas kernels, local(): pl.pallas_call(lambda *refs: kernel(n_space, n_tm, *refs), out_shape=jax....  49.7 us

profile of v5, /device:TPU:1, one launch (start us, length us, event | category | flops | bytes accessed | tf_op | source)
XLA Modules:
  0.0 50.2 jit_solution(17352417203932886705)
XLA Ops:
  0.0 49.7 %loops.1 = f32[2,1,33]{2,1,0:T(1,128)S(1)} custom-call(f32[2,2,4,3,8,128]{5,4,3,2,1,0:T(8,128)} %bitcast.10, f32[2,2,6,6,8,128]{5,4,3,2,1,0:T(8,128)} %bitcast.8, f32[4,2,3,3,8,128]{5,4,3,2,1,0:T(8,128)} %bitcast.9, s32[3,33]{1,0:T(4,128)} %bitcast.11), custom_call_target="tpu_custom_call" | custom-call | tf_op jit(solution)/shard_map/loops/pallas_call | solution.py:653
  49.7 0.6 %copy.7 = f32[2,1,33,1]{2,3,1,0:T(1,128)} copy(f32[2,1,33,1]{2,3,1,0:T(1,128)S(1)} %bitcast.7) | data formatting | bytes 528
